TPU v7x, 128 devices: a whole 4x4x4 slice. The times are simulated.
128 devices in a mesh: adapter: 32 (over x, z, core), head: 4 (over y).
Axes of the slice: x: 4, y: 4, z: 4, core: 2. Of those that a mesh axis runs over, the one named last changes fastest.
Arguments:
- call_token_inputs: bfloat16 [1024, 32, 4096], P('adapter', None, 'head'), may hold values from -6 to 6
- routed_group_index: int32 [1024], replicated, may hold values from 0 to 31, as said below
- call_adapter_index: int32 [1024, 1], replicated, may hold values from 0 to 63
- holder_table_row: int32 [64], replicated, may hold values from 0 to 63, each once
- channel_input_weight: bfloat16 [4096, 4096], P(None, 'head'), may hold values from -0.09375 to 0.09375
- input_state_weight: bfloat16 [4096, 512], P(None, 'head'), may hold values from -0.09375 to 0.09375
- output_state_weight: bfloat16 [4096, 512], P(None, 'head'), may hold values from -0.09375 to 0.09375
- step_size_weight: bfloat16 [4096, 64], P(None, 'head'), may hold values from -0.09375 to 0.09375
- channel_input_taps: bfloat16 [4, 4096], P(None, 'head'), may hold values from -3 to 3
- input_state_taps: bfloat16 [4, 512], P(None, 'head'), may hold values from -3 to 3
- output_state_taps: bfloat16 [4, 512], P(None, 'head'), may hold values from -3 to 3
- adapter_down_weight: bfloat16 [64, 4096, 64], P('adapter', None, 'head'), may hold values from -0.09375 to 0.09375
- adapter_up_weight: bfloat16 [64, 64, 4096], P('adapter', None, 'head'), may hold values from -0.75 to 0.75
- decay_logarithm: float32 [64], P('head'), may hold values from -2.5 to 1.5
- step_size_bias: float32 [64], P('head'), may hold values from -2 to 0
- head_skip_factor: float32 [64], P('head'), may hold values from 0.5 to 1.5
Outputs:
- replies: bfloat16 [2048, 32, 4096], P('adapter', None, 'head')
Inputs may be any that keep to these rules, and one draw needn't show every extreme that they name: `routed_group_index`: among the 32 calls of one source no group is named more than 2 times, and one group is named exactly 2 times by every source. `call_adapter_index`: every adapter is named by some call. `holder_table_row`: A permutation of 0 to 63.
All inputs are finite; a program needn't handle non-finite values.
Results may differ from a plain program's by a relative error of at most 0.0035.
Values may be sent and summed in bfloat16 or wider, within the bound.
A program may use at most 192 MiB of HBM per device.

v0:
```python
import jax
import jax.numpy as jnp
from jax import lax
from jax.sharding import PartitionSpec as P

HEAD_DIM = 64
NSTATE = 128
CAP = 2


PRECISE = lax.Precision.HIGHEST


def call_ranks(group_grid):
    count = group_grid.shape[-1]
    same_group = group_grid[..., :, None] == group_grid[..., None, :]
    earlier = jnp.arange(count)[None, :] < jnp.arange(count)[:, None]
    return jnp.sum(jnp.where(same_group & earlier, 1, 0), axis=-1).astype(jnp.int32)


def causal_filter_apply(series, kernel):
    span = kernel.shape[0]
    length = series.shape[1]
    padded = jnp.pad(series, ((0, 0), (span - 1, 0), (0, 0)))
    summed = jnp.zeros(series.shape, jnp.float32)
    for offset in range(span):
        summed = (
            summed + kernel[offset].astype(jnp.float32) * padded[:, offset : offset + length, :]
        )
    return jax.nn.silu(summed)


def state_space(
    filtered_inputs, b_conv, c_conv, dt_vals, decay_logarithm, head_skip_factor, call_token_length
):
    blocks = filtered_inputs.shape[0]
    block_rows = filtered_inputs.shape[1]
    head_count = decay_logarithm.shape[0]
    group_count = b_conv.shape[2] // NSTATE
    x_heads = filtered_inputs.reshape(blocks, block_rows, head_count, HEAD_DIM)
    b_groups = b_conv.reshape(blocks, block_rows, group_count, NSTATE)
    c_groups = c_conv.reshape(blocks, block_rows, group_count, NSTATE)
    step_vals = -jnp.exp(decay_logarithm) * dt_vals
    cumulated = jnp.cumsum(jnp.moveaxis(step_vals, 2, 1), axis=2)
    row_iota = jnp.arange(block_rows)
    causal = (row_iota[:, None] // call_token_length == row_iota[None, :] // call_token_length) & (
        row_iota[None, :] <= row_iota[:, None]
    )
    segment = cumulated[:, :, :, None] - cumulated[:, :, None, :]
    decay = jnp.where(causal, jnp.exp(jnp.where(causal, segment, 0.0)), 0.0)
    routing_marks = jnp.einsum("ntgk,njgk->ngtj", c_groups, b_groups, precision=PRECISE)
    routing_marks = jnp.repeat(routing_marks, head_count // group_count, axis=1)
    mixing = routing_marks * decay * jnp.moveaxis(dt_vals, 2, 1)[:, :, None, :]
    output = (
        jnp.einsum("nhtj,njhp->nthp", mixing, x_heads, precision=PRECISE)
        + head_skip_factor[:, None] * x_heads
    )
    return output.reshape(blocks, block_rows, head_count * HEAD_DIM)


def on_device(
    call_token_inputs,
    routed_group_index,
    call_adapter_index,
    holder_table_row,
    channel_input_weight,
    input_state_weight,
    output_state_weight,
    step_size_weight,
    channel_input_taps,
    input_state_taps,
    output_state_taps,
    adapter_down_weight,
    adapter_up_weight,
    decay_logarithm,
    step_size_bias,
    head_skip_factor,
):
    sender_indices = lax.axis_size("adapter")
    my_group = lax.axis_index("adapter")
    per_source = call_token_inputs.shape[0]
    call_token_length = call_token_inputs.shape[1]
    slot_count = sender_indices * CAP
    group_grid = routed_group_index.reshape(sender_indices, per_source)
    rank_grid = call_ranks(group_grid)
    call_iota = jnp.arange(per_source, dtype=jnp.int32)
    my_groups = lax.dynamic_index_in_dim(group_grid, my_group, 0, keepdims=False)
    my_ranks = lax.dynamic_index_in_dim(rank_grid, my_group, 0, keepdims=False)
    send_slot = my_groups * CAP + my_ranks
    slot_iota = jnp.arange(slot_count, dtype=jnp.int32)
    send_match = send_slot[None, :] == slot_iota[:, None]
    send_live = jnp.any(send_match, axis=1)
    send_call = jnp.sum(jnp.where(send_match, call_iota[None, :], 0), axis=1)
    rank_iota = jnp.arange(CAP, dtype=jnp.int32)
    recv_match = (group_grid[:, None, :] == my_group) & (
        rank_grid[:, None, :] == rank_iota[None, :, None]
    )
    local_call = jnp.sum(jnp.where(recv_match, call_iota[None, None, :], 0), axis=2)
    global_call = (
        jnp.arange(sender_indices, dtype=jnp.int32)[:, None] * per_source + local_call
    ).reshape(-1)
    slot_pos = holder_table_row[call_adapter_index[global_call, 0]]
    down_weight_table, up_weight_table = (
        lax.all_gather(adapter_down_weight, "adapter", axis=0, tiled=True),
        lax.all_gather(adapter_up_weight, "adapter", axis=0, tiled=True),
    )
    slot_down_weight = jnp.take(down_weight_table, slot_pos, axis=0)
    slot_up_weight = jnp.take(up_weight_table, slot_pos, axis=0)
    features = lax.all_gather(call_token_inputs, "head", axis=2, tiled=True)
    outgoing = jnp.where(
        send_live[:, None, None],
        jnp.take(features, send_call, axis=0),
        jnp.zeros((), features.dtype),
    )
    landed_rows = lax.all_to_all(outgoing, "adapter", split_axis=0, concat_axis=0, tiled=True)
    flat_rows = landed_rows.reshape(-1, landed_rows.shape[2])
    projected_inputs = jnp.dot(flat_rows, channel_input_weight, preferred_element_type=jnp.float32)
    proj_b = jnp.dot(flat_rows, input_state_weight, preferred_element_type=jnp.float32)
    proj_c = jnp.dot(flat_rows, output_state_weight, preferred_element_type=jnp.float32)
    proj_dt = jnp.dot(flat_rows, step_size_weight, preferred_element_type=jnp.float32)
    reduced_features = jnp.einsum(
        "vxg,vgj->vxj", landed_rows, slot_down_weight, preferred_element_type=jnp.float32
    )
    local_slot_count = landed_rows.shape[0]
    reduced_every_call = lax.all_gather(
        reduced_features.astype(jnp.bfloat16), "head", axis=2, tiled=True
    )
    adapter_delta_output = jnp.einsum(
        "uce,ued->ucd", reduced_every_call, slot_up_weight, preferred_element_type=jnp.float32
    )
    filtered_inputs = causal_filter_apply(
        projected_inputs.reshape(local_slot_count, call_token_length, -1) + adapter_delta_output,
        channel_input_taps,
    )
    b_conv = causal_filter_apply(
        proj_b.reshape(local_slot_count, call_token_length, -1), input_state_taps
    )
    c_conv = causal_filter_apply(
        proj_c.reshape(local_slot_count, call_token_length, -1), output_state_taps
    )
    dt_vals = jax.nn.softplus(
        proj_dt.reshape(local_slot_count, call_token_length, -1) + step_size_bias
    )
    row_total = local_slot_count * call_token_length
    block_rows = min(128, row_total)
    blocks = row_total // block_rows

    def blocked(values):
        return values.reshape(blocks, block_rows, values.shape[2])

    output = state_space(
        blocked(filtered_inputs),
        blocked(b_conv),
        blocked(c_conv),
        blocked(dt_vals),
        decay_logarithm,
        head_skip_factor,
        call_token_length,
    )
    return output.reshape(local_slot_count, call_token_length, -1).astype(jnp.bfloat16)


def solution(mesh):
    placed = (
        P("adapter", None, "head"),
        P(),
        P(),
        P(),
        P(None, "head"),
        P(None, "head"),
        P(None, "head"),
        P(None, "head"),
        P(None, "head"),
        P(None, "head"),
        P(None, "head"),
        P("adapter", None, "head"),
        P("adapter", None, "head"),
        P("head"),
        P("head"),
        P("head"),
    )
    return jax.shard_map(
        on_device, mesh=mesh, in_specs=placed, out_specs=P("adapter", None, "head"), check_vma=False
    )
```

profile of v0, /device:TPU:44, one launch (start us, length us, event | category | flops | bytes accessed | tf_op | source)
XLA Modules:
  0.0 619.1 jit_solution(13992757347904840570)
XLA Ops:
  10.5 83.5 %all-gather.4.cloned.1.call-done = bf16[32,32,4096]{2,1,0:T(8,128)(2,1)} async-done(((bf16[32,32,1024]{2,1,0:T(8,128)(2,1)}), bf16[32,32,4096]{2,1,0:T(8,128)(2,1)}) %all-gather.4.cloned.1.call-update) | async-done | bytes 8388624 | tf_op jit(solution)/shard_map/all_gather | solution.py:109
  94.1 10.9 %gather_fusion = bf16[64,32,4096]{2,1,0:T(8,128)(2,1)} fusion(bf16[32,32,4096]{2,1,0:T(8,128)(2,1)} %all-gather.4.cloned.1.call-done, s32[1024]{0:T(1024)S(1)} %pad_clamp_fusion.2), kind=kCustom, calls=%fused_computation | custom fusion | bytes 33554688 | tf_op jit(solution)/shard_map/jit(_take)/gather | solution.py:112
  104.9 14.4 %select_select_fusion = bf16[64,32,4096]{2,1,0:T(8,128)(2,1)} fusion(bf16[64,32,4096]{2,1,0:T(8,128)(2,1)} %gather_fusion, pred[64]{0:T(512)(128)(4,1)S(1)} %compare_and_fusion.1, pred[64]{0:T(512)(128)(4,1)S(1)} %fusion.57), kind=kLoop, calls=%fused_computation.12 | loop fusion | flops 16777216 | bytes 33554560 | tf_op jit(solution)/shard_map/jit(_where)/select_n | solution.py:110
  119.4 7.7 %all-to-all-start = ((bf16[64,32,4096]{2,1,0:T(8,128)(2,1)}), bf16[64,32,4096]{2,1,0:T(8,128)(2,1)}, u32[]{:S(2)}, u32[]{:S(2)}) async-start(bf16[64,32,4096]{2,1,0:T(8,128)(2,1)} %select_select_fusion), calls=%async_computation | async-start | bytes 33554432 | tf_op jit(solution)/shard_map/all_to_all | solution.py:115
  132.1 149.8 %all-gather.6.cloned.1.call-done = bf16[64,4096,16]{1,2,0:T(8,128)(2,1)} async-done(((bf16[2,4096,16]{1,2,0:T(8,128)(2,1)}), bf16[64,4096,16]{1,2,0:T(8,128)(2,1)}) %all-gather.6.cloned.1.call-update) | async-done | bytes 8388624 | tf_op jit(solution)/shard_map/all_gather | solution.py:104
  281.9 8.9 %gather_fusion.3 = bf16[64,4096,16]{1,2,0:T(8,128)(2,1)} fusion(bf16[64,4096,16]{1,2,0:T(8,128)(2,1)} %all-gather.6.cloned.1.call-done, s32[1024]{0:T(1024)S(1)} %pad_clamp_fusion), kind=kCustom, calls=%fused_computation.3 | custom fusion | bytes 16777472 | tf_op jit(solution)/shard_map/jit(_take)/gather | solution.py:107
  290.8 105.7 %all-gather.8.cloned.1.call-done = bf16[64,64,1024]{2,1,0:T(8,128)(2,1)} async-done(((bf16[2,64,1024]{2,1,0:T(8,128)(2,1)}), bf16[64,64,1024]{2,1,0:T(8,128)(2,1)}) %all-gather.8.cloned.1.call-update) | async-done | bytes 8388624 | tf_op jit(solution)/shard_map/all_gather | solution.py:105
  396.4 8.9 %gather_fusion.4 = bf16[64,64,1024]{2,1,0:T(8,128)(2,1)} fusion(bf16[64,64,1024]{2,1,0:T(8,128)(2,1)} %all-gather.8.cloned.1.call-done, s32[1024]{0:T(1024)S(1)} %pad_clamp_fusion), kind=kCustom, calls=%fused_computation.4 | custom fusion | bytes 16777472 | tf_op jit(solution)/shard_map/jit(_take)/gather | solution.py:108
  405.3 8.6 %all-to-all-done = bf16[64,32,4096]{2,1,0:T(8,128)(2,1)} async-done(((bf16[64,32,4096]{2,1,0:T(8,128)(2,1)}), bf16[64,32,4096]{2,1,0:T(8,128)(2,1)}, u32[]{:S(2)}, u32[]{:S(2)}) %all-to-all-start) | async-done | bytes 16777248 | tf_op jit(solution)/shard_map/all_to_all | solution.py:115
  413.9 10.5 %fusion.35 = bf16[64,32,16]{1,2,0:T(8,128)(2,1)S(1)} fusion(bf16[64,32,4096]{2,1,0:T(8,128)(2,1)} %all-to-all-done, bf16[64,4096,16]{1,2,0:T(8,128)(2,1)} %gather_fusion.3, pred[64]{0:T(512)(128)(4,1)S(1)} %compare_and_fusion), kind=kOutput, calls=%fused_computation.50 | convolution fusion | flops 272662528 | bytes 25231424 | tf_op jit(solution)/shard_map/vxg,vgj->vxj/dot_general | solution.py:121
  424.5 15.8 %all_gather.14 = bf16[64,32,64]{1,2,0:T(8,128)(2,1)S(1)} all-gather(bf16[64,32,16]{1,2,0:T(8,128)(2,1)S(1)} %fusion.35), channel_id=1, replica_groups=mesh['adapter'=32,'head'=4] {'head'}, dimensions={2}, use_global_device_ids=true | all-gather | bytes 327680 | tf_op jit(solution)/shard_map/all_gather | solution.py:125
  440.3 4.8 fusion.21
  445.1 24.3 %fusion.32 = f32[64,32,1024]{2,1,0:T(8,128)} fusion(f32[64,32,1024]{2,1,0:T(8,128)S(1)} %fusion.21, bf16[64,32,4096]{2,1,0:T(8,128)(2,1)} %all-to-all-done, bf16[4096,1024]{1,0:T(8,128)(2,1)} %param.20), kind=kOutput, calls=%fused_computation.41 | convolution fusion | flops 17181966336 | bytes 41943040 | tf_op jit(solution)/shard_map/dot_general | solution.py:117
  469.4 16.3 %divide_multiply_fusion = f32[64,32,1024]{2,1,0:T(8,128)} fusion(f32[64,32,1024]{2,1,0:T(8,128)} %fusion.32, f32[1024]{0:T(1024)S(1)} %bitcast.85, f32[1024]{0:T(1024)S(1)} %bitcast.86, f32[1024]{0:T(1024)S(1)} %bitcast.84, f32[1024]{0:T(1024)S(1)} %bitcast.83), kind=kLoop, calls=%fused_computation.31 | loop fusion | flops 23068672 | bytes 16793600 | tf_op jit(solution)/shard_map/jit(silu)/mul | solution.py:30
  485.7 13.3 %reshape_reshape.2 = f32[16,128,16,64]{3,2,1,0:T(8,128)} reshape(f32[64,32,1024]{2,1,0:T(8,128)} %divide_multiply_fusion) | data formatting | bytes 16777216 | tf_op jit(solution)/shard_map/reshape;reshape | solution.py:40
  499.0 13.4 %copy.35 = f32[16,128,16,64]{1,3,2,0:T(8,128)} copy(f32[16,128,16,64]{3,2,1,0:T(8,128)} %reshape_reshape.2) | data formatting | bytes 16777216 | tf_op jit(solution)/shard_map/reshape;reshape | solution.py:40
  512.4 14.7 %compare_select_fusion = f32[64,32,16]{1,2,0:T(8,128)S(1)} fusion(bf16[64,32,4096]{2,1,0:T(8,128)(2,1)} %all-to-all-done, f32[16]{0:T(128)S(1)} %copy-done.12, bf16[4096,16]{0,1:T(8,128)(2,1)S(1)} %copy-done.3), kind=kOutput, calls=%fused_computation.42 | convolution fusion | flops 268664832 | bytes 17039424 | tf_op jit(solution)/shard_map/dot_general | solution.py:120
  527.7 8.3 %fusion.52 = f32[64,32,128]{2,1,0:T(8,128)S(1)} fusion(bf16[64,32,4096]{2,1,0:T(8,128)(2,1)} %all-to-all-done, bf16[4096,128]{1,0:T(8,128)(2,1)S(1)} %copy-done), kind=kOutput, calls=%fused_computation.65 | convolution fusion | flops 2147483648 | bytes 18874368 | tf_op jit(solution)/shard_map/dot_general | solution.py:119
  536.8 8.2 %fusion.50 = f32[64,32,128]{2,1,0:T(8,128)S(1)} fusion(bf16[64,32,4096]{2,1,0:T(8,128)(2,1)} %all-to-all-done, bf16[4096,128]{1,0:T(8,128)(2,1)S(1)} %copy-done.22), kind=kOutput, calls=%fused_computation.63 | convolution fusion | flops 2147483648 | bytes 18874368 | tf_op jit(solution)/shard_map/dot_general | solution.py:118
  545.6 2.3 fusion.67
  547.9 4.5 reduce_window_sum.11
  552.5 38.2 %fusion.13 = bf16[16,128,16,64]{1,3,2,0:T(8,128)(2,1)} fusion(f32[16,128,16,64]{1,3,2,0:T(8,128)} %copy.35, f32[16]{0:T(128)S(1)} %copy-done.24, f32[16,16,128]{2,1,0:T(8,128)S(1)} %copy.34, f32[16,16,128]{2,1,0:T(8,128)S(1)} %reduce_window_sum.11, f32[16,128,128]{2,1,0:T(8,128)S(1)} %fusion.67, pred[128,128]{1,0:T(8,128)(4,1)S(1)} %copy-done.9), kind=kOutput, calls=%fused_computation.23 | convolution fusion | flops 3248488448 | bytes 13910080 | tf_op jit(solution)/shard_map/nhtj,njhp->nthp/dot_general | solution.py:55
  590.7 10.1 %copy.37 = bf16[16,128,16,64]{3,2,1,0:T(8,128)(2,1)} copy(bf16[16,128,16,64]{1,3,2,0:T(8,128)(2,1)} %fusion.13) | data formatting | bytes 8388608 | tf_op jit(solution)/shard_map/convert_element_type | solution.py:160
  600.8 11.9 %convert_element_type.160 = bf16[64,32,1024]{2,1,0:T(8,128)(2,1)} reshape(bf16[16,128,16,64]{3,2,1,0:T(8,128)(2,1)} %copy.37) | data formatting | bytes 8388608 | tf_op jit(solution)/shard_map/convert_element_type | solution.py:160
  (92 shorter events, 10.8 us)
Async XLA Ops:
  6.5 521.2 %copy-start = (bf16[4096,128]{1,0:T(8,128)(2,1)S(1)}, bf16[4096,128]{1,0:T(8,128)(2,1)}, u32[]{:S(2)}) copy-start(bf16[4096,128]{1,0:T(8,128)(2,1)} %param.22) | copy-start | bytes 3145732
  6.5 87.5 %all-gather.4.cloned.1.call-start = ((), (), s32[]{:S(2)}) async-start(), calls=%async_computation.1 | async-start | bytes 10485760 | tf_op jit(solution)/shard_map/all_gather | solution.py:109
  7.3 274.6 %all-gather.6.cloned.1.call-start = ((), (), s32[]{:S(2)}) async-start(), calls=%async_computation.2 | async-start | bytes 8650752 | tf_op jit(solution)/shard_map/all_gather | solution.py:104
  8.0 388.4 %all-gather.8.cloned.1.call-start = ((), (), s32[]{:S(2)}) async-start(), calls=%async_computation.3 | async-start | bytes 8650752 | tf_op jit(solution)/shard_map/all_gather | solution.py:105
  119.3 8.9 %copy-start.1 = (s32[64]{0:T(128)S(1)}, s32[64]{0:T(128)}, u32[]{:S(2)}) copy-start(s32[64]{0:T(128)} %param.19) | copy-start | bytes 772
  119.3 9.7 %copy-start.23 = (f32[16]{0:T(128)S(1)}, f32[16]{0:T(128)}, u32[]{:S(2)}) copy-start(f32[16]{0:T(128)} %param.29) | copy-start | bytes 196
  119.3 10.3 %copy-start.10 = (bf16[4,128]{1,0:T(4,128)(2,1)S(1)}, bf16[4,128]{1,0:T(4,128)(2,1)}, u32[]{:S(2)}) copy-start(bf16[4,128]{1,0:T(4,128)(2,1)} %param.26) | copy-start | bytes 3076
  119.3 10.8 %copy-start.11 = (bf16[4,128]{1,0:T(4,128)(2,1)S(1)}, bf16[4,128]{1,0:T(4,128)(2,1)}, u32[]{:S(2)}) copy-start(bf16[4,128]{1,0:T(4,128)(2,1)} %param.25) | copy-start | bytes 3076
  119.3 12.1 %copy-start.4 = (bf16[4,1024]{1,0:T(4,128)(2,1)S(1)}, bf16[4,1024]{1,0:T(4,128)(2,1)}, u32[]{:S(2)}) copy-start(bf16[4,1024]{1,0:T(4,128)(2,1)} %param.24) | copy-start | bytes 24580
  119.4 294.6 %all-to-all-start = ((bf16[64,32,4096]{2,1,0:T(8,128)(2,1)}), bf16[64,32,4096]{2,1,0:T(8,128)(2,1)}, u32[]{:S(2)}, u32[]{:S(2)}) async-start(bf16[64,32,4096]{2,1,0:T(8,128)(2,1)} %select_select_fusion), calls=%async_computation | async-start | bytes 33554432 | tf_op jit(solution)/shard_map/all_to_all | solution.py:115
  445.1 24.3 %copy-start.5 = (f32[1,1024]{1,0:T(1,128)S(1)}, f32[1,1024]{1,0:T(1,128)}, u32[]{:S(2)}) copy-start(f32[1,1024]{1,0:T(1,128)} %get-tuple-element.5) | copy-start | bytes 12292
  445.1 24.3 %copy-start.6 = (f32[1,1024]{1,0:T(1,128)S(1)}, f32[1,1024]{1,0:T(1,128)}, u32[]{:S(2)}) copy-start(f32[1,1024]{1,0:T(1,128)} %get-tuple-element.6) | copy-start | bytes 12292
  445.1 24.3 %copy-start.7 = (f32[1,1024]{1,0:T(1,128)S(1)}, f32[1,1024]{1,0:T(1,128)}, u32[]{:S(2)}) copy-start(f32[1,1024]{1,0:T(1,128)} %get-tuple-element.7) | copy-start | bytes 12292
  445.1 24.3 %copy-start.8 = (f32[1,1024]{1,0:T(1,128)S(1)}, f32[1,1024]{1,0:T(1,128)}, u32[]{:S(2)}) copy-start(f32[1,1024]{1,0:T(1,128)} %get-tuple-element.8) | copy-start | bytes 12292
  499.0 13.4 %copy-start.3 = (bf16[4096,16]{0,1:T(8,128)(2,1)S(1)}, bf16[4096,16]{0,1:T(8,128)(2,1)}, u32[]{:S(2)}) copy-start(bf16[4096,16]{0,1:T(8,128)(2,1)} %param.23) | copy-start | bytes 393220
  499.0 13.4 %copy-start.12 = (f32[16]{0:T(128)S(1)}, f32[16]{0:T(128)}, u32[]{:S(2)}) copy-start(f32[16]{0:T(128)} %param.30) | copy-start | bytes 196
  512.4 15.1 %copy-start.21 = (f32[16]{0:T(128)S(1)}, f32[16]{0:T(128)}, u32[]{:S(2)}) copy-start(f32[16]{0:T(128)} %exponential_negate_fusion) | copy-start | bytes 196
  527.7 8.3 %copy-start.17 = (f32[128]{0:T(128)S(1)}, f32[128]{0:T(128)}, u32[]{:S(2)}) copy-start(f32[128]{0:T(128)} %get-tuple-element.13) | copy-start | bytes 1540
  527.7 8.3 %copy-start.18 = (f32[128]{0:T(128)S(1)}, f32[128]{0:T(128)}, u32[]{:S(2)}) copy-start(f32[128]{0:T(128)} %get-tuple-element.14) | copy-start | bytes 1540
  527.7 8.3 %copy-start.19 = (f32[128]{0:T(128)S(1)}, f32[128]{0:T(128)}, u32[]{:S(2)}) copy-start(f32[128]{0:T(128)} %get-tuple-element.15) | copy-start | bytes 1540
  527.7 8.3 %copy-start.20 = (f32[128]{0:T(128)S(1)}, f32[128]{0:T(128)}, u32[]{:S(2)}) copy-start(f32[128]{0:T(128)} %get-tuple-element.16) | copy-start | bytes 1540
  527.7 8.9 %copy-start.22 = (bf16[4096,128]{1,0:T(8,128)(2,1)S(1)}, bf16[4096,128]{1,0:T(8,128)(2,1)}, u32[]{:S(2)}) copy-start(bf16[4096,128]{1,0:T(8,128)(2,1)} %param.21) | copy-start | bytes 3145732
  536.7 15.7 %copy-start.9 = (pred[128,128]{1,0:T(8,128)(4,1)S(1)}, pred[128,128]{1,0:T(8,128)(4,1)}, u32[]{:S(2)}) copy-start(pred[128,128]{1,0:T(8,128)(4,1)} %fusion.55) | copy-start | bytes 49156
  536.7 15.7 %copy-start.24 = (f32[16]{0:T(128)S(1)}, f32[16]{0:T(128)}, u32[]{:S(2)}) copy-start(f32[16]{0:T(128)} %param.31) | copy-start | bytes 196
  (5 other events, 41.1 us)
Sparse Core Ops, SparseCore 0:
  9.0 84.9 all-gather.3
  96.3 185.5 all-gather.5
  284.1 112.2 all-gather.7
where the time goes:
time: 620 us; the launch traced here: 619 us
  waiting for transfers between devices  350 us (56%)
  matrix products  111 us (18%)
  local copies, waits for them, and re-layouts  80.4 us (13%)
  other arithmetic  40.8 us (7%)
  blocking collectives  15.8 us (3%)
  between operations  13.6 us (2%)
  starting transfers between devices  7.74 us (1%)
    all_gather x1, waiting for transfers between devices, on_device(): lax.all_gather(adapter_down_weight, 'adapter', axis=0, tiled=True)  150 us
    all_gather x1, waiting for transfers between devices, on_device(): lax.all_gather(adapter_up_weight, 'adapter', axis=0, tiled=True)  106 us
    all_gather x1, waiting for transfers between devices, on_device(): features = lax.all_gather(call_token_inputs, 'head', axis=2, tiled=True)  83.5 us
    dot_general x1, matrix products, state_space(): jnp.einsum('nhtj,njhp->nthp', mixing, x_heads, precision=PRECISE)  38.2 us
    another operation x2, local copies, waits for them, and re-layouts, state_space(): x_heads = filtered_inputs.reshape(blocks, block_rows, head_count, HEAD_DIM)  26.7 us
    dot_general x1, matrix products, on_device(): jnp.dot(flat_rows, channel_input_weight, preferred_element_type=jnp.float32)  24.3 us
    convert_element_type x2, local copies, waits for them, and re-layouts, on_device(): output.reshape(local_slot_count, call_token_length, -1).astype(jnp.bfloat16)  21.9 us
    mul x3, other arithmetic, causal_filter_apply(): return jax.nn.silu(summed)  17.5 us
  transfers between devices with their start and end apart: 4, of which 4 were waited for; matrix products, arithmetic and copies ran while one was open for 8% of the time, Pallas kernels for 0%

commit v1 on v0

v1 whole, which is shorter than its diff:
```python
import functools

import jax
import jax.numpy as jnp
from jax import lax
from jax.experimental import pallas as pl
from jax.experimental.pallas import tpu as pltpu
from jax.sharding import PartitionSpec as P

HEAD_DIM = 64
NSTATE = 128
CAP = 2
CHUNK = 4
PAD = 8
RING = 4
MESH = pl.DeviceIdType.MESH
HIGH = lax.Precision.HIGHEST
F32 = jnp.float32
BF16 = jnp.bfloat16

OFFSETS = (0, -1, 1, 2)
N_TABLE = 4 + 16 + 16


def nt_dot(a, b):
    return lax.dot_general(a, b, (((1,), (1,)), ((), ())), preferred_element_type=F32)


class Table:
    def __init__(self, buf, send, recv, first, second, core, strides, axes_to_adapter):
        self.buf, self.send, self.recv = buf, send, recv
        self.first, self.second, self.core = first, second, core
        self.strides = strides
        self.to_adapter = axes_to_adapter

    def owner(self, df, ds, core=None):
        core = self.core if core is None else core
        a = lax.rem(self.first + (df + RING), RING)
        b = lax.rem(self.second + (ds + RING), RING)
        return a * self.strides[0] + b * self.strides[1] + core

    def unit(self, df, ds, part=None, core=None):
        ref = self.buf.at[self.owner(df, ds, core)]
        return ref if part is None else ref.at[part]

    def copy(self, ref, index, target):
        return pltpu.make_async_remote_copy(
            src_ref=ref,
            dst_ref=ref,
            send_sem=self.send.at[index],
            recv_sem=self.recv.at[index],
            device_id={"adapter": target},
            device_id_type=MESH,
        )

    def plain(self, df):
        return 0 if df is None else 4 + 4 * OFFSETS.index(df)

    def send_plain(self, df):
        base = self.plain(df)
        if df is None:
            self.copy(self.unit(0, 0), base, self.owner(1, 0)).start()
            self.copy(self.unit(0, 0), base + 1, self.owner(-1, 0)).start()
        else:
            self.copy(self.unit(df, 0), base, self.owner(0, 1)).start()
            self.copy(self.unit(df, 0), base + 1, self.owner(0, -1)).start()

    def got_plain(self, df):
        base = self.plain(df)
        here = self.owner(0, 0)
        if df is None:
            self.copy(self.unit(-1, 0), base, here).wait_recv()
            self.copy(self.unit(1, 0), base + 1, here).wait_recv()
        else:
            self.copy(self.unit(df, -1), base, here).wait_recv()
            self.copy(self.unit(df, 1), base + 1, here).wait_recv()

    def send_relay(self, df):
        base = self.plain(df) + 2
        if df is None:
            self.copy(self.unit(-1, 0, 0), base, self.owner(1, 0)).start()
            self.copy(self.unit(1, 0, 1), base + 1, self.owner(-1, 0)).start()
        else:
            self.copy(self.unit(df, -1, 0), base, self.owner(0, 1)).start()
            self.copy(self.unit(df, 1, 1), base + 1, self.owner(0, -1)).start()

    def got_relay(self, df):
        base = self.plain(df) + 2
        here = self.owner(0, 0)
        at = (2, 0) if df is None else (df, 2)
        self.copy(self.unit(*at, 0), base, here).wait_recv()
        self.copy(self.unit(*at, 1), base + 1, here).wait_recv()

    def twin_index(self, df, ds):
        return 20 + 4 * OFFSETS.index(df) + OFFSETS.index(ds)

    def send_twin(self, df, ds):
        self.copy(
            self.unit(df, ds), self.twin_index(df, ds), self.owner(0, 0, 1 - self.core)
        ).start()

    def got_twins(self):
        here = self.owner(0, 0)
        for df in OFFSETS:
            for ds in OFFSETS:
                self.copy(
                    self.unit(df, ds, core=1 - self.core), self.twin_index(df, ds), here
                ).wait_recv()

    def sent_all(self):
        here = self.owner(0, 0)
        for df in (None, *OFFSETS):
            base = self.plain(df)
            for i in (0, 1):
                self.copy(self.unit(0, 0), base + i, here).wait_send()
                self.copy(self.unit(0, 0, 0), base + 2 + i, here).wait_send()
        for i in range(16):
            self.copy(self.unit(0, 0), 20 + i, here).wait_send()

    def event(self, number):
        if number == 0:
            self.send_plain(None)
            self.send_plain(0)
            self.send_twin(0, 0)
        elif number == 1:
            self.got_plain(None)
            self.send_relay(None)
            self.send_plain(-1)
            self.send_plain(1)
            self.got_plain(0)
            self.send_relay(0)
            for at in ((-1, 0), (1, 0), (0, -1), (0, 1)):
                self.send_twin(*at)
        elif number == 2:
            self.got_relay(None)
            self.send_plain(2)
            self.send_twin(2, 0)
            self.got_relay(0)
            self.send_twin(0, 2)
        elif number == 3:
            for df in (-1, 1):
                self.got_plain(df)
                self.send_relay(df)
                self.send_twin(df, -1)
                self.send_twin(df, 1)
        elif number == 4:
            self.got_plain(2)
            self.send_relay(2)
            self.send_twin(2, -1)
            self.send_twin(2, 1)
            for df in (-1, 1):
                self.got_relay(df)
                self.send_twin(df, 2)
        elif number == 5:
            self.got_relay(2)
            self.send_twin(2, 2)


N_EVENTS = 6


def mixer_kernel(
    meta,
    params,
    taps,
    skip,
    wdt_in,
    x_hbm,
    wx_hbm,
    wb_hbm,
    wc_hbm,
    down_hbm,
    up_hbm,
    out_hbm,
    x_in,
    x_all,
    w_all,
    wdt,
    down,
    up,
    proj,
    proj_dt,
    low,
    gathered,
    done,
    slots,
    load_sem,
    y_send,
    y_recv,
    table_send,
    table_recv,
    low_send,
    low_recv,
    out_send,
    out_recv,
):
    sources = lax.axis_size("adapter")
    me = lax.axis_index("adapter")
    y = lax.axis_index("head")
    calls, length, width = x_in.shape
    chunks = calls // CHUNK
    rows = CHUNK * length
    cols = wx_hbm.shape[1]
    half = CHUNK // 2
    right, left = lax.rem(y + 1, RING), lax.rem(y + RING - 1, RING)
    across = lax.rem(y + 2, RING)
    core = lax.rem(me, 2)
    pos_z = lax.rem(lax.div(me, 2), RING)
    pos_x = lax.div(me, 2 * RING)

    loads = [
        pltpu.make_async_copy(x_hbm, x_in, load_sem.at[0]),
        pltpu.make_async_copy(down_hbm, down.at[me], load_sem.at[1]),
        pltpu.make_async_copy(up_hbm, up.at[me], load_sem.at[2]),
        pltpu.make_async_copy(wx_hbm, w_all.at[:, pl.ds(0, cols)], load_sem.at[3]),
        pltpu.make_async_copy(wb_hbm, w_all.at[:, pl.ds(cols, NSTATE)], load_sem.at[4]),
        pltpu.make_async_copy(
            wc_hbm, w_all.at[:, pl.ds(cols + NSTATE, NSTATE)], load_sem.at[5]
        ),
    ]
    for load in loads:
        load.start()

    barrier = pltpu.get_barrier_semaphore()

    def greet(i, carry):
        pl.semaphore_signal(
            barrier,
            inc=1,
            device_id={"adapter": lax.rem(me + i, sources)},
            device_id_type=MESH,
        )
        return carry

    lax.fori_loop(1, sources, greet, 0)
    for d in range(1, RING):
        pl.semaphore_signal(
            barrier,
            inc=1,
            device_id={"head": lax.rem(y + d, RING)},
            device_id_type=MESH,
        )
    pl.semaphore_wait(barrier, sources - 1 + RING - 1)

    table_down = Table(
        down, table_send.at[0], table_recv.at[0], pos_x, pos_z, core, (2 * RING, 2), None
    )
    table_up = Table(
        up, table_send.at[1], table_recv.at[1], pos_z, pos_x, core, (2, 2 * RING), None
    )
    tables = (table_down, table_up)

    loads[1].wait()
    loads[2].wait()
    for table in tables:
        table.event(0)

    loads[0].wait()

    def arrange(j, carry):
        x_all[y, j] = x_in[meta[0, j]]
        return carry

    lax.fori_loop(0, calls, arrange, 0)

    def y_copy(kind, owner, k, target):
        if kind < 2:
            ref = x_all.at[owner, pl.ds(k * CHUNK, CHUNK)]
        else:
            ref = x_all.at[owner, pl.ds(k * CHUNK + (kind - 2) * half, half)]
        return pltpu.make_async_remote_copy(
            src_ref=ref,
            dst_ref=ref,
            send_sem=y_send.at[kind, k],
            recv_sem=y_recv.at[kind, k],
            device_id={"head": target},
            device_id_type=MESH,
        )

    def send_own(k):
        y_copy(0, y, k, right).start()
        y_copy(1, y, k, left).start()

    send_own(0)
    send_own(1)

    for k in range(chunks):
        for c in range(CHUNK):
            proj[k, c, pl.ds(0, PAD), :] = jnp.zeros((PAD, proj.shape[3]), F32)
    wdt[...] = jnp.zeros(wdt.shape, BF16)
    wdt[:, pl.ds(0, wdt_in.shape[1])] = wdt_in[...]
    loads[3].wait()
    loads[4].wait()
    loads[5].wait()

    def chunk_tokens(owner, k):
        return x_all[owner, pl.ds(k * CHUNK, CHUNK)].reshape(rows, width)

    tile = 256 if (cols + 2 * NSTATE) % 256 == 0 else 128

    def first_loop(k, carry):
        y_copy(0, left, k, y).wait_recv()
        y_copy(2, left, k, right).start()
        y_copy(1, right, k, y).wait_recv()
        y_copy(3, right, k, left).start()

        @pl.when(k + 2 < chunks)
        def _():
            send_own(k + 2)

        for number in range(1, N_EVENTS):

            @pl.when(k == number)
            def _(number=number):
                for table in tables:
                    table.event(number)

        y_copy(2, across, k, y).wait_recv()
        y_copy(3, across, k, y).wait_recv()

        @pl.loop(0, w_all.shape[1] // tile)
        def _(n):
            at = pl.ds(pl.multiple_of(n * tile, tile), tile)
            total = jnp.zeros((rows, tile), F32)
            for owner in range(RING):
                total = total + jnp.dot(
                    chunk_tokens(owner, k),
                    w_all[pl.ds(owner * width, width), at],
                    preferred_element_type=F32,
                )
            proj[k, :, pl.ds(PAD, length), at] = total.reshape(CHUNK, length, tile)

        total = jnp.zeros((rows, wdt.shape[1]), F32)
        for owner in range(RING):
            total = total + jnp.dot(
                chunk_tokens(owner, k),
                wdt[pl.ds(owner * width, width), :],
                preferred_element_type=F32,
            )
        proj_dt[k] = total
        return carry

    lax.fori_loop(0, chunks, first_loop, 0)

    for table in tables:
        table.got_twins()

    rank = down.shape[2]

    def low_copy(owner, d, k, target):
        ref = low.at[owner, k]
        return pltpu.make_async_remote_copy(
            src_ref=ref,
            dst_ref=ref,
            send_sem=low_send.at[d - 1, k],
            recv_sem=low_recv.at[d - 1, k],
            device_id={"head": target},
            device_id_type=MESH,
        )

    def down_loop(k, carry):
        for c in range(CHUNK):
            row = meta[1, k * CHUNK + c]
            gathered[pl.ds(c * rank, rank), :] = down[lax.div(row, 2), lax.rem(row, 2)]
        total = jnp.zeros((rows, CHUNK * rank), F32)
        for owner in range(RING):
            total = total + nt_dot(
                chunk_tokens(owner, k), gathered[:, pl.ds(owner * width, width)]
            )
        row_call = lax.broadcasted_iota(jnp.int32, total.shape, 0) // length
        lane_call = lax.broadcasted_iota(jnp.int32, total.shape, 1) // rank
        kept = jnp.where(row_call == lane_call, total, 0.0).astype(BF16)
        shape = (CHUNK * rank, low.shape[3])
        from_rank = lax.broadcasted_iota(jnp.int32, shape, 0) % rank + y * rank
        fold = jnp.where(
            from_rank == lax.broadcasted_iota(jnp.int32, shape, 1), 1.0, 0.0
        ).astype(BF16)
        low[y, k] = jnp.dot(kept, fold, preferred_element_type=F32).astype(BF16)
        for d in range(1, RING):
            low_copy(y, d, k, lax.rem(y + d, RING)).start()
        return carry

    lax.fori_loop(0, chunks, down_loop, 0)

    def out_copy(i, target, source):
        return pltpu.make_async_remote_copy(
            src_ref=slots.at[pl.ds(i * CAP, CAP)],
            dst_ref=out_hbm.at[pl.ds(source * CAP, CAP)],
            send_sem=out_send.at[i],
            recv_sem=out_recv.at[i],
            device_id={"adapter": target},
            device_id_type=MESH,
        )

    def fill(i):
        for r in range(CAP):
            at = i * CAP + r
            block = done[meta[2, at]].astype(F32)
            slots[at] = jnp.where(meta[3, at] > 0, block, 0.0).astype(BF16)

    def send_slots(i):
        fill(i)
        out_copy(i, lax.rem(me + i, sources), me).start()

    own = pltpu.make_async_copy(
        slots.at[pl.ds(0, CAP)], out_hbm.at[pl.ds(me * CAP, CAP)], load_sem.at[6]
    )

    decay_rate = -jnp.exp(params[0:1, :])
    bias = params[1:2, :]
    rank_all = up.shape[2]

    def conv(k, at):
        total = jnp.zeros((CHUNK, length, 128), F32)
        for i in range(4):
            total = total + taps[pl.ds(i, 1), at].reshape(1, 1, 128) * proj[
                k, :, pl.ds(PAD - 3 + i, length), at
            ]
        total = total.reshape(rows, 128)
        return total / (1.0 + jnp.exp(-total))

    def mix_loop(k, carry):
        for d in range(1, RING):
            low_copy(lax.rem(y + RING - d, RING), d, k, y).wait_recv()
        low_rank = (
            low[0, k].astype(F32)
            + low[1, k].astype(F32)
            + low[2, k].astype(F32)
            + low[3, k].astype(F32)
        ).astype(BF16)
        for c in range(CHUNK):
            row = meta[1, k * CHUNK + c]
            weight = up[lax.div(row, 2), lax.rem(row, 2)]
            delta = jnp.dot(
                low_rank[c * length : (c + 1) * length, :rank_all],
                weight,
                preferred_element_type=F32,
            )
            proj[k, c, pl.ds(PAD, length), pl.ds(0, cols)] = (
                proj[k, c, pl.ds(PAD, length), pl.ds(0, cols)] + delta
            )
        t_iota = lax.broadcasted_iota(jnp.int32, (rows, rows), 0)
        j_iota = lax.broadcasted_iota(jnp.int32, (rows, rows), 1)
        causal = (t_iota // length == j_iota // length) & (j_iota <= t_iota)
        raw = proj_dt[k] + bias
        dt = jnp.maximum(raw, 0.0) + jnp.log1p(jnp.exp(-jnp.abs(raw)))
        cum = jnp.dot(
            jnp.where(causal, 1.0, 0.0),
            decay_rate * dt,
            preferred_element_type=F32,
            precision=HIGH,
        )
        cum_t = cum.T
        dt_t = dt.T
        b_conv = conv(k, pl.ds(cols, NSTATE))
        c_conv = conv(k, pl.ds(cols + NSTATE, NSTATE))
        marks = lax.dot_general(
            c_conv,
            b_conv,
            (((1,), (1,)), ((), ())),
            preferred_element_type=F32,
            precision=HIGH,
        )
        lane = lax.broadcasted_iota(jnp.int32, (rows, 128), 1)
        for pair in range(cols // 128):
            at = pl.ds(pair * 128, 128)
            x_conv = conv(k, at)
            mixing = []
            for h in (2 * pair, 2 * pair + 1):
                segment = cum[:, h : h + 1] - cum_t[h : h + 1, :]
                decay = jnp.exp(jnp.where(causal, segment, -1e30))
                mixing.append((marks * decay * dt_t[h : h + 1, :]).astype(BF16))
            x_low = jnp.where(lane < HEAD_DIM, x_conv, 0.0).astype(BF16)
            x_high = jnp.where(lane < HEAD_DIM, 0.0, x_conv).astype(BF16)
            mixed = jnp.dot(
                jnp.concatenate(mixing, axis=1),
                jnp.concatenate([x_low, x_high], axis=0),
                preferred_element_type=F32,
            )
            mixed = mixed + skip[0:1, at] * x_conv
            done[pl.ds(k * CHUNK, CHUNK), :, at] = mixed.reshape(
                CHUNK, length, 128
            ).astype(BF16)

        @pl.when(k == 0)
        def _():
            fill(0)
            own.start()

        @pl.when(k > 0)
        def _():
            send_slots(2 * k)

        send_slots(2 * k + 1)
        return carry

    lax.fori_loop(0, chunks, mix_loop, 0)

    def rest_loop(i, carry):
        send_slots(i)
        return carry

    lax.fori_loop(calls // CAP, sources, rest_loop, 0)

    own.wait()
    for table in tables:
        table.sent_all()

    def drain(k, carry):
        for kind in range(4):
            y_copy(kind, y, k, y).wait_send()
        for d in range(1, RING):
            low_copy(y, d, k, y).wait_send()
        return carry

    lax.fori_loop(0, chunks, drain, 0)

    def drain_out(i, carry):
        out_copy(i, me, me).wait_send()
        out_copy(i, me, lax.rem(me + sources - i, sources)).wait_recv()
        return carry

    lax.fori_loop(1, sources, drain_out, 0)


def routing(routed_group_index, call_adapter_index, holder_table_row, me, sources, calls):
    group = lax.dynamic_slice(routed_group_index, (me * calls,), (calls,))
    named = lax.dynamic_slice(call_adapter_index[:, 0], (me * calls,), (calls,))
    call = jnp.arange(calls, dtype=jnp.int32)
    same = group[:, None] == group[None, :]
    rank = jnp.sum(jnp.where(same & (call[None, :] < call[:, None]), 1, 0), axis=1)
    key = lax.rem(group - me + sources, sources) * CAP + rank
    place = jnp.sum(jnp.where(key[None, :] < key[:, None], 1, 0), axis=1)
    row = jnp.sum(
        jnp.where(
            named[:, None] == jnp.arange(holder_table_row.shape[0], dtype=jnp.int32)[None, :],
            holder_table_row[None, :],
            0,
        ),
        axis=1,
    )
    slot = jnp.arange(sources * CAP, dtype=jnp.int32)
    here = place[None, :] == slot[:, None]
    order = jnp.sum(jnp.where(here, call[None, :], 0), axis=1)
    rows = jnp.sum(jnp.where(here, row[None, :], 0), axis=1)
    taken = jnp.sum(jnp.where(key[None, :] < slot[:, None], 1, 0), axis=1)
    live = jnp.sum(jnp.where(key[None, :] == slot[:, None], 1, 0), axis=1)
    return jnp.stack([order, rows, jnp.minimum(taken, calls - 1), live]).astype(jnp.int32)


def on_device(
    call_token_inputs,
    routed_group_index,
    call_adapter_index,
    holder_table_row,
    channel_input_weight,
    input_state_weight,
    output_state_weight,
    step_size_weight,
    channel_input_taps,
    input_state_taps,
    output_state_taps,
    adapter_down_weight,
    adapter_up_weight,
    decay_logarithm,
    step_size_bias,
    head_skip_factor,
):
    sources = lax.axis_size("adapter")
    me = lax.axis_index("adapter")
    calls, length, width = call_token_inputs.shape
    cols = channel_input_weight.shape[1]
    heads = decay_logarithm.shape[0]
    chunks = calls // CHUNK
    rows = CHUNK * length
    total_cols = cols + 2 * NSTATE
    meta = routing(
        routed_group_index, call_adapter_index, holder_table_row, me, sources, calls
    )
    params = jnp.stack([decay_logarithm, step_size_bias])
    params = jnp.pad(params, ((0, 6), (0, 128 - heads)))
    taps = jnp.concatenate(
        [channel_input_taps, input_state_taps, output_state_taps], axis=1
    ).astype(F32)
    skip = jnp.broadcast_to(head_skip_factor[:, None], (heads, HEAD_DIM)).reshape(1, cols)
    down = jnp.swapaxes(adapter_down_weight, 1, 2)
    per_owner, rank, depth = down.shape
    rank_all = adapter_up_weight.shape[1]
    vmem = pl.BlockSpec(memory_space=pltpu.VMEM)
    anywhere = pl.BlockSpec(memory_space=pl.ANY)
    dma = pltpu.SemaphoreType.DMA
    return pl.pallas_call(
        mixer_kernel,
        out_shape=jax.ShapeDtypeStruct((sources * CAP, length, cols), BF16),
        in_specs=[pl.BlockSpec(memory_space=pltpu.SMEM)] + [vmem] * 4 + [anywhere] * 6,
        out_specs=anywhere,
        scratch_shapes=[
            pltpu.VMEM((calls, length, width), BF16),
            pltpu.VMEM((RING, calls, length, width), BF16),
            pltpu.VMEM((depth, total_cols), BF16),
            pltpu.VMEM((depth, 128), BF16),
            pltpu.VMEM((sources, per_owner, rank, depth), BF16),
            pltpu.VMEM((sources, per_owner, rank_all, cols), BF16),
            pltpu.VMEM((chunks, CHUNK, PAD + length, total_cols), F32),
            pltpu.VMEM((chunks, rows, 128), F32),
            pltpu.VMEM((RING, chunks, rows, 128), BF16),
            pltpu.VMEM((CHUNK * rank, depth), BF16),
            pltpu.VMEM((calls, length, cols), BF16),
            pltpu.VMEM((sources * CAP, length, cols), BF16),
            dma((7,)),
            dma((4, chunks)),
            dma((4, chunks)),
            dma((2, N_TABLE)),
            dma((2, N_TABLE)),
            dma((RING - 1, chunks)),
            dma((RING - 1, chunks)),
            dma((sources,)),
            dma((sources,)),
        ],
        compiler_params=pltpu.CompilerParams(
            collective_id=0, has_side_effects=True, vmem_limit_bytes=60 * 2**20
        ),
        cost_estimate=pl.CostEstimate(
            flops=2 * calls * length * depth * (total_cols + 128),
            bytes_accessed=30 * 2**20,
            transcendentals=calls * length * rows * heads,
        ),
    )(
        meta,
        params,
        taps,
        skip,
        step_size_weight,
        call_token_inputs,
        channel_input_weight,
        input_state_weight,
        output_state_weight,
        down,
        adapter_up_weight,
    )


def solution(mesh):
    placed = (
        P("adapter", None, "head"),
        P(),
        P(),
        P(),
        P(None, "head"),
        P(None, "head"),
        P(None, "head"),
        P(None, "head"),
        P(None, "head"),
        P(None, "head"),
        P(None, "head"),
        P("adapter", None, "head"),
        P("adapter", None, "head"),
        P("head"),
        P("head"),
        P("head"),
    )
    return jax.shard_map(
        on_device, mesh=mesh, in_specs=placed, out_specs=P("adapter", None, "head"), check_vma=False
    )
```

time: 620 us -> 175 us (0.28)
  the two profiles are of different devices: /device:TPU:44 before, /device:TPU:101 now
where the time goes in v1:
time: 175 us; the launch traced here: 174 us
  Pallas kernels  159 us (91%)
  local copies, waits for them, and re-layouts  10.2 us (6%)
  other arithmetic  5.35 us (3%)
    pallas_call x1, Pallas kernels, on_device(): pl.pallas_call(mixer_kernel, out_shape=jax.ShapeDtypeStruct((sources * CA...  159 us
    unnamed x4, local copies, waits for them, and re-layouts  7.92 us

profile of v1, /device:TPU:101, one launch (start us, length us, event | category | flops | bytes accessed | tf_op | source)
XLA Modules:
  0.0 174.2 jit_solution(11031729893409768329)
XLA Ops:
  0.0 0.0 copy-start
  0.0 0.7 copy-done
  0.7 0.1 dynamic-slice_bitcast_fusion
  0.8 0.8 select_reduce_fusion.3
  1.6 0.8 dynamic_slice.6
  2.4 0.2 select_reduce_fusion.6
  2.5 0.8 fusion.3
  3.3 0.2 select_reduce_fusion.5
  3.5 0.1 select_reduce_fusion.4
  3.6 0.1 select_reduce_fusion.1
  3.7 0.6 pad_add_fusion.meta
  4.3 1.3 select_maximum_fusion.params
  5.6 0.7 broadcast_in_dim.79
  6.3 0.7 reshape.22.skip
  7.0 1.3 maximum_convert_fusion.taps
  8.3 2.2 %copy.18.wdt_in = bf16[4096,16]{1,0:T(8,128)(2,1)} copy(bf16[4096,16]{0,1:T(8,128)(2,1)} %param.23) | data formatting | bytes 262144 | tf_op args[7]
  10.5 158.7 %shard_map.154 = bf16[64,32,1024]{2,1,0:T(8,128)(2,1)} custom-call(s32[4,64]{1,0:T(4,128)} %pad_add_fusion.meta, f32[8,128]{1,0:T(8,128)} %select_maximum_fusion.params, f32[4,1280]{1,0:T(4,128)} %maximum_convert_fusion.taps, f32[1,1024]{1,0:T(1,128)} %reshape.22.skip, bf16[4096,16]{1,0:T(8,128)(2,1)} %copy.18.wdt_in, bf16[32,32,1024]{2,1,0:T(8,128)(2,1)} %x_hbm.1, ...), custom_call_target="tpu_custom_call" | custom-call | flops 11811160064 | bytes 31457280 | tf_op jit(solution)/shard_map/pallas_call | solution.py:592
  169.2 5.0 %copy.20 = bf16[64,32,1024]{2,1,0:T(8,128)(2,1)} copy(bf16[64,32,1024]{2,1,0:T(8,128)(2,1)} %shard_map.154) | data formatting | bytes 8388608
  (1 shorter events, 0.0 us)
Async XLA Ops:
  0.0 0.7 copy-start

commit v2 on v1

--- a/solution.py
+++ b/solution.py
@@ -20,6 +20,13 @@
 
 OFFSETS = (0, -1, 1, 2)
 N_TABLE = 4 + 16 + 16
+
+CHIP_STEPS = (
+    (2, 1), (1, 2), (2, 3), (3, 2), (2, 2), (2, 0), (0, 2), (1, 1),
+    (3, 3), (1, 3), (3, 1), (1, 0), (0, 1), (3, 0), (0, 3), (0, 0),
+)
+STEPS = tuple((dx, dz, dc) for dx, dz in CHIP_STEPS for dc in (0, 1))
+TABLES_AT = 5
 
 
 def nt_dot(a, b):
@@ -179,10 +186,10 @@
     down,
     up,
     proj,
-    proj_dt,
+    between,
+    mixing,
     low,
     gathered,
-    done,
     slots,
     load_sem,
     y_send,
@@ -284,68 +291,86 @@
     send_own(0)
     send_own(1)
 
-    for k in range(chunks):
-        for c in range(CHUNK):
-            proj[k, c, pl.ds(0, PAD), :] = jnp.zeros((PAD, proj.shape[3]), F32)
+    for c in range(CHUNK):
+        between[c, pl.ds(0, PAD), :] = jnp.zeros((PAD, 2 * NSTATE), F32)
+        for k in range(chunks):
+            proj[k, c, pl.ds(0, PAD), :] = jnp.zeros((PAD, cols), F32)
     wdt[...] = jnp.zeros(wdt.shape, BF16)
     wdt[:, pl.ds(0, wdt_in.shape[1])] = wdt_in[...]
     loads[3].wait()
     loads[4].wait()
     loads[5].wait()
 
+    done = x_in
+    rank = down.shape[2]
+    rank_all = up.shape[2]
+    decay_rate = -jnp.exp(params[0:1, :])
+    bias = params[1:2, :]
+
     def chunk_tokens(owner, k):
         return x_all[owner, pl.ds(k * CHUNK, CHUNK)].reshape(rows, width)
 
-    tile = 256 if (cols + 2 * NSTATE) % 256 == 0 else 128
-
-    def first_loop(k, carry):
-        y_copy(0, left, k, y).wait_recv()
-        y_copy(2, left, k, right).start()
-        y_copy(1, right, k, y).wait_recv()
-        y_copy(3, right, k, left).start()
-
-        @pl.when(k + 2 < chunks)
-        def _():
-            send_own(k + 2)
-
-        for number in range(1, N_EVENTS):
-
-            @pl.when(k == number)
-            def _(number=number):
-                for table in tables:
-                    table.event(number)
-
-        y_copy(2, across, k, y).wait_recv()
-        y_copy(3, across, k, y).wait_recv()
-
-        @pl.loop(0, w_all.shape[1] // tile)
+    def project(k, weight, at):
+        total = None
+        for owner in range(RING):
+            term = jnp.dot(
+                chunk_tokens(owner, k),
+                weight[pl.ds(owner * width, width), at],
+                preferred_element_type=F32,
+            )
+            total = term if total is None else total + term
+        return total
+
+    def conv(series, at, taps_at):
+        total = jnp.zeros((CHUNK, length, 128), F32)
+        for i in range(4):
+            total = total + taps[pl.ds(i, 1), taps_at].reshape(1, 1, 128) * series[
+                :, pl.ds(PAD - 3 + i, length), at
+            ]
+        total = total.reshape(rows, 128)
+        return total / (1.0 + jnp.exp(-total))
+
+    def before_adapters(k):
+        tile = 256 if cols % 256 == 0 else 128
+
+        @pl.loop(0, cols // tile)
         def _(n):
             at = pl.ds(pl.multiple_of(n * tile, tile), tile)
-            total = jnp.zeros((rows, tile), F32)
-            for owner in range(RING):
-                total = total + jnp.dot(
-                    chunk_tokens(owner, k),
-                    w_all[pl.ds(owner * width, width), at],
-                    preferred_element_type=F32,
-                )
-            proj[k, :, pl.ds(PAD, length), at] = total.reshape(CHUNK, length, tile)
-
-        total = jnp.zeros((rows, wdt.shape[1]), F32)
-        for owner in range(RING):
-            total = total + jnp.dot(
-                chunk_tokens(owner, k),
-                wdt[pl.ds(owner * width, width), :],
-                preferred_element_type=F32,
+            proj[k, :, pl.ds(PAD, length), at] = project(k, w_all, at).reshape(
+                CHUNK, length, tile
             )
-        proj_dt[k] = total
-        return carry
-
-    lax.fori_loop(0, chunks, first_loop, 0)
-
-    for table in tables:
-        table.got_twins()
-
-    rank = down.shape[2]
+
+        between[:, pl.ds(PAD, length), :] = project(
+            k, w_all, pl.ds(cols, 2 * NSTATE)
+        ).reshape(CHUNK, length, 2 * NSTATE)
+        raw = project(k, wdt, slice(None)) + bias
+        t_iota = lax.broadcasted_iota(jnp.int32, (rows, rows), 0)
+        j_iota = lax.broadcasted_iota(jnp.int32, (rows, rows), 1)
+        causal = (t_iota // length == j_iota // length) & (j_iota <= t_iota)
+        dt = jnp.maximum(raw, 0.0) + jnp.log1p(jnp.exp(-jnp.abs(raw)))
+        cum = jnp.dot(
+            jnp.where(causal, 1.0, 0.0),
+            decay_rate * dt,
+            preferred_element_type=F32,
+            precision=HIGH,
+        )
+        cum_t = cum.T
+        dt_t = dt.T
+        b_conv = conv(between, pl.ds(0, NSTATE), pl.ds(cols, NSTATE))
+        c_conv = conv(between, pl.ds(NSTATE, NSTATE), pl.ds(cols + NSTATE, NSTATE))
+        marks = lax.dot_general(
+            c_conv,
+            b_conv,
+            (((1,), (1,)), ((), ())),
+            preferred_element_type=F32,
+            precision=HIGH,
+        )
+        for h in range(cols // HEAD_DIM):
+            segment = cum[:, h : h + 1] - cum_t[h : h + 1, :]
+            decay = jnp.exp(jnp.where(causal, segment, -1e30))
+            mixing[k, h // 2, :, pl.ds((h % 2) * rows, rows)] = (
+                marks * decay * dt_t[h : h + 1, :]
+            ).astype(BF16)
 
     def low_copy(owner, d, k, target):
         ref = low.at[owner, k]
@@ -358,7 +383,7 @@
             device_id_type=MESH,
         )
 
-    def down_loop(k, carry):
+    def reduce_chunk(k, carry):
         for c in range(CHUNK):
             row = meta[1, k * CHUNK + c]
             gathered[pl.ds(c * rank, rank), :] = down[lax.div(row, 2), lax.rem(row, 2)]
@@ -380,7 +405,13 @@
             low_copy(y, d, k, lax.rem(y + d, RING)).start()
         return carry
 
-    lax.fori_loop(0, chunks, down_loop, 0)
+    def at_step(i, sign):
+        dx, dz, dc = STEPS[i]
+        return (
+            lax.rem(pos_x + (sign * dx) % RING, RING) * (2 * RING)
+            + lax.rem(pos_z + (sign * dz) % RING, RING) * 2
+            + lax.rem(core + dc, 2)
+        )
 
     def out_copy(i, target, source):
         return pltpu.make_async_remote_copy(
@@ -392,34 +423,24 @@
             device_id_type=MESH,
         )
 
-    def fill(i):
+    at_home = STEPS.index((0, 0, 0))
+    own = pltpu.make_async_copy(
+        slots.at[pl.ds(at_home * CAP, CAP)],
+        out_hbm.at[pl.ds(me * CAP, CAP)],
+        load_sem.at[6],
+    )
+
+    def send_slots(i):
         for r in range(CAP):
             at = i * CAP + r
             block = done[meta[2, at]].astype(F32)
             slots[at] = jnp.where(meta[3, at] > 0, block, 0.0).astype(BF16)
-
-    def send_slots(i):
-        fill(i)
-        out_copy(i, lax.rem(me + i, sources), me).start()
-
-    own = pltpu.make_async_copy(
-        slots.at[pl.ds(0, CAP)], out_hbm.at[pl.ds(me * CAP, CAP)], load_sem.at[6]
-    )
-
-    decay_rate = -jnp.exp(params[0:1, :])
-    bias = params[1:2, :]
-    rank_all = up.shape[2]
-
-    def conv(k, at):
-        total = jnp.zeros((CHUNK, length, 128), F32)
-        for i in range(4):
-            total = total + taps[pl.ds(i, 1), at].reshape(1, 1, 128) * proj[
-                k, :, pl.ds(PAD - 3 + i, length), at
-            ]
-        total = total.reshape(rows, 128)
-        return total / (1.0 + jnp.exp(-total))
-
-    def mix_loop(k, carry):
+        if i == at_home:
+            own.start()
+        else:
+            out_copy(i, at_step(i, 1), me).start()
+
+    def after_adapters(k, carry):
         for d in range(1, RING):
             low_copy(lax.rem(y + RING - d, RING), d, k, y).wait_recv()
         low_rank = (
@@ -436,71 +457,77 @@
                 weight,
                 preferred_element_type=F32,
             )
-            proj[k, c, pl.ds(PAD, length), pl.ds(0, cols)] = (
-                proj[k, c, pl.ds(PAD, length), pl.ds(0, cols)] + delta
-            )
-        t_iota = lax.broadcasted_iota(jnp.int32, (rows, rows), 0)
-        j_iota = lax.broadcasted_iota(jnp.int32, (rows, rows), 1)
-        causal = (t_iota // length == j_iota // length) & (j_iota <= t_iota)
-        raw = proj_dt[k] + bias
-        dt = jnp.maximum(raw, 0.0) + jnp.log1p(jnp.exp(-jnp.abs(raw)))
-        cum = jnp.dot(
-            jnp.where(causal, 1.0, 0.0),
-            decay_rate * dt,
-            preferred_element_type=F32,
-            precision=HIGH,
-        )
-        cum_t = cum.T
-        dt_t = dt.T
-        b_conv = conv(k, pl.ds(cols, NSTATE))
-        c_conv = conv(k, pl.ds(cols + NSTATE, NSTATE))
-        marks = lax.dot_general(
-            c_conv,
-            b_conv,
-            (((1,), (1,)), ((), ())),
-            preferred_element_type=F32,
-            precision=HIGH,
-        )
+            proj[k, c, pl.ds(PAD, length), :] = proj[k, c, pl.ds(PAD, length), :] + delta
         lane = lax.broadcasted_iota(jnp.int32, (rows, 128), 1)
         for pair in range(cols // 128):
             at = pl.ds(pair * 128, 128)
-            x_conv = conv(k, at)
-            mixing = []
-            for h in (2 * pair, 2 * pair + 1):
-                segment = cum[:, h : h + 1] - cum_t[h : h + 1, :]
-                decay = jnp.exp(jnp.where(causal, segment, -1e30))
-                mixing.append((marks * decay * dt_t[h : h + 1, :]).astype(BF16))
-            x_low = jnp.where(lane < HEAD_DIM, x_conv, 0.0).astype(BF16)
-            x_high = jnp.where(lane < HEAD_DIM, 0.0, x_conv).astype(BF16)
-            mixed = jnp.dot(
-                jnp.concatenate(mixing, axis=1),
-                jnp.concatenate([x_low, x_high], axis=0),
-                preferred_element_type=F32,
-            )
-            mixed = mixed + skip[0:1, at] * x_conv
+            x_conv = conv(proj.at[k], at, at)
+            x_high = x_conv.astype(BF16)
+            mixed = skip[0:1, at] * x_conv
+            for part in (x_high.astype(F32), x_conv - x_high.astype(F32)):
+                first = jnp.where(lane < HEAD_DIM, part, 0.0).astype(BF16)
+                second = jnp.where(lane < HEAD_DIM, 0.0, part).astype(BF16)
+                mixed = mixed + jnp.dot(
+                    mixing[k, pair],
+                    jnp.concatenate([first, second], axis=0),
+                    preferred_element_type=F32,
+                )
             done[pl.ds(k * CHUNK, CHUNK), :, at] = mixed.reshape(
                 CHUNK, length, 128
             ).astype(BF16)
-
-        @pl.when(k == 0)
+        for number in range(chunks):
+
+            @pl.when(k == number)
+            def _(number=number):
+                for i in range(CHUNK // CAP):
+                    send_slots(number * (CHUNK // CAP) + i)
+
+        return carry
+
+    last = chunks - 1
+
+    def step(k, carry):
+        y_copy(0, left, k, y).wait_recv()
+        y_copy(2, left, k, right).start()
+        y_copy(1, right, k, y).wait_recv()
+        y_copy(3, right, k, left).start()
+
+        @pl.when(k + 2 < chunks)
         def _():
-            fill(0)
-            own.start()
-
-        @pl.when(k > 0)
+            send_own(k + 2)
+
+        for number in range(1, N_EVENTS):
+
+            @pl.when(k == number)
+            def _(number=number):
+                for table in tables:
+                    table.event(number)
+
+        lax.fori_loop(4, jnp.where(k == last, last - 1, 4), after_adapters, 0)
+        y_copy(2, across, k, y).wait_recv()
+        y_copy(3, across, k, y).wait_recv()
+        before_adapters(k)
+
+        @pl.when(k == TABLES_AT)
         def _():
-            send_slots(2 * k)
-
-        send_slots(2 * k + 1)
+            for table in tables:
+                table.got_twins()
+
+        lax.fori_loop(
+            jnp.where(k == TABLES_AT, 0, k), jnp.where(k >= TABLES_AT, k + 1, k), reduce_chunk, 0
+        )
+        lax.fori_loop(
+            jnp.where(k == last, last - 1, 0),
+            jnp.where(k == last, chunks, jnp.where(k == last - 1, 4, 0)),
+            after_adapters,
+            0,
+        )
         return carry
 
-    lax.fori_loop(0, chunks, mix_loop, 0)
-
-    def rest_loop(i, carry):
+    lax.fori_loop(0, chunks, step, 0)
+
+    for i in range(calls // CAP, sources):
         send_slots(i)
-        return carry
-
-    lax.fori_loop(calls // CAP, sources, rest_loop, 0)
 
     own.wait()
     for table in tables:
@@ -514,13 +541,10 @@
         return carry
 
     lax.fori_loop(0, chunks, drain, 0)
-
-    def drain_out(i, carry):
-        out_copy(i, me, me).wait_send()
-        out_copy(i, me, lax.rem(me + sources - i, sources)).wait_recv()
-        return carry
-
-    lax.fori_loop(1, sources, drain_out, 0)
+    for i in range(sources):
+        if i != at_home:
+            out_copy(i, me, me).wait_send()
+            out_copy(i, me, at_step(i, -1)).wait_recv()
 
 
 def routing(routed_group_index, call_adapter_index, holder_table_row, me, sources, calls):
@@ -529,7 +553,19 @@
     call = jnp.arange(calls, dtype=jnp.int32)
     same = group[:, None] == group[None, :]
     rank = jnp.sum(jnp.where(same & (call[None, :] < call[:, None]), 1, 0), axis=1)
-    key = lax.rem(group - me + sources, sources) * CAP + rank
+    way = (
+        lax.rem(group // (2 * RING) - me // (2 * RING) + RING, RING) * (2 * RING)
+        + lax.rem((group // 2) % RING - (me // 2) % RING + RING, RING) * 2
+        + lax.rem(group % 2 + me % 2, 2)
+    )
+    step_ways = jnp.array([dx * 2 * RING + dz * 2 + dc for dx, dz, dc in STEPS], jnp.int32)
+    step = jnp.sum(
+        jnp.where(
+            way[:, None] == step_ways[None, :], jnp.arange(sources, dtype=jnp.int32)[None, :], 0
+        ),
+        axis=1,
+    )
+    key = step * CAP + rank
     place = jnp.sum(jnp.where(key[None, :] < key[:, None], 1, 0), axis=1)
     row = jnp.sum(
         jnp.where(
@@ -601,11 +637,11 @@
             pltpu.VMEM((depth, 128), BF16),
             pltpu.VMEM((sources, per_owner, rank, depth), BF16),
             pltpu.VMEM((sources, per_owner, rank_all, cols), BF16),
-            pltpu.VMEM((chunks, CHUNK, PAD + length, total_cols), F32),
-            pltpu.VMEM((chunks, rows, 128), F32),
+            pltpu.VMEM((chunks, CHUNK, PAD + length, cols), F32),
+            pltpu.VMEM((CHUNK, PAD + length, 2 * NSTATE), F32),
+            pltpu.VMEM((chunks, cols // 128, rows, 2 * rows), BF16),
             pltpu.VMEM((RING, chunks, rows, 128), BF16),
             pltpu.VMEM((CHUNK * rank, depth), BF16),
-            pltpu.VMEM((calls, length, cols), BF16),
             pltpu.VMEM((sources * CAP, length, cols), BF16),
             dma((7,)),
             dma((4, chunks)),

time: 175 us -> 163 us (0.931)
  the two profiles are of different devices: /device:TPU:101 before, /device:TPU:1 now
where the time goes in v2:
time: 163 us; the launch traced here: 161 us
  Pallas kernels  146 us (90%)
  local copies, waits for them, and re-layouts  8.71 us (5%)
  other arithmetic  6.05 us (4%)
    pallas_call x1, Pallas kernels, on_device(): pl.pallas_call(mixer_kernel, out_shape=jax.ShapeDtypeStruct((sources * CA...  146 us
    unnamed x4, local copies, waits for them, and re-layouts  7.23 us

profile of v2, /device:TPU:1, one launch (start us, length us, event | category | flops | bytes accessed | tf_op | source)
XLA Modules:
  0.0 161.2 jit_solution(18299541552882574511)
XLA Ops:
  0.0 0.0 copy-start
  0.0 0.8 fusion.7
  0.8 0.0 copy-done
  0.8 0.1 dynamic-slice_bitcast_fusion
  0.9 0.8 select_reduce_fusion.3
  1.7 0.8 select_reduce_fusion.6
  2.6 0.2 select_reduce_fusion.5
  2.8 0.1 select_reduce_fusion.4
  2.9 0.1 select_reduce_fusion.1
  3.0 0.6 pad_add_fusion.meta
  3.6 1.3 select_maximum_fusion.params
  4.8 0.7 broadcast_in_dim.96
  5.5 0.7 reshape.34.skip
  6.2 1.3 maximum_convert_fusion.taps
  7.6 2.2 %copy.19.wdt_in = bf16[4096,16]{1,0:T(8,128)(2,1)} copy(bf16[4096,16]{0,1:T(8,128)(2,1)} %param.24) | data formatting | bytes 262144 | tf_op args[7]
  9.8 146.5 %shard_map.163 = bf16[64,32,1024]{2,1,0:T(8,128)(2,1)} custom-call(s32[4,64]{1,0:T(4,128)} %pad_add_fusion.meta, f32[8,128]{1,0:T(8,128)} %select_maximum_fusion.params, f32[4,1280]{1,0:T(4,128)} %maximum_convert_fusion.taps, f32[1,1024]{1,0:T(1,128)} %reshape.34.skip, bf16[4096,16]{1,0:T(8,128)(2,1)} %copy.19.wdt_in, bf16[32,32,1024]{2,1,0:T(8,128)(2,1)} %x_hbm.1, ...), custom_call_target="tpu_custom_call" | custom-call | flops 11811160064 | bytes 31457280 | tf_op jit(solution)/shard_map/pallas_call | solution.py:628
  156.2 5.0 %copy.21 = bf16[64,32,1024]{2,1,0:T(8,128)(2,1)} copy(bf16[64,32,1024]{2,1,0:T(8,128)(2,1)} %shard_map.163) | data formatting | bytes 8388608
  (2 shorter events, 0.0 us)
Async XLA Ops:
  0.0 0.8 copy-start

commit v3 on v2

--- a/solution.py
+++ b/solution.py
@@ -22,11 +22,14 @@
 N_TABLE = 4 + 16 + 16
 
 CHIP_STEPS = (
-    (2, 1), (1, 2), (2, 3), (3, 2), (2, 2), (2, 0), (0, 2), (1, 1),
-    (3, 3), (1, 3), (3, 1), (1, 0), (0, 1), (3, 0), (0, 3), (0, 0),
+    ((2, 1), (2, 3), (1, 2), (3, 2)),
+    ((2, 2), (2, 0), (0, 2)),
+    ((1, 1), (3, 3), (1, 3), (3, 1)),
+    ((1, 0), (3, 0), (0, 1), (0, 3)),
+    ((0, 0),),
 )
-STEPS = tuple((dx, dz, dc) for dx, dz in CHIP_STEPS for dc in (0, 1))
-TABLES_AT = 5
+STEPS = tuple((dx, dz, dc) for group in CHIP_STEPS for dc in (1, 0) for dx, dz in group)
+TABLES_AT = 6
 
 
 def nt_dot(a, b):
@@ -407,10 +410,12 @@
 
     def at_step(i, sign):
         dx, dz, dc = STEPS[i]
+        other = lax.rem(core + dc, 2)
+        side = sign * (1 - 2 * (core if sign == 1 else other))
         return (
-            lax.rem(pos_x + (sign * dx) % RING, RING) * (2 * RING)
-            + lax.rem(pos_z + (sign * dz) % RING, RING) * 2
-            + lax.rem(core + dc, 2)
+            lax.rem(pos_x + side * dx + RING, RING) * (2 * RING)
+            + lax.rem(pos_z + side * dz + RING, RING) * 2
+            + other
         )
 
     def out_copy(i, target, source):
@@ -486,45 +491,49 @@
 
     last = chunks - 1
 
-    def step(k, carry):
-        y_copy(0, left, k, y).wait_recv()
-        y_copy(2, left, k, right).start()
-        y_copy(1, right, k, y).wait_recv()
-        y_copy(3, right, k, left).start()
-
-        @pl.when(k + 2 < chunks)
+    def step(t, carry):
+        @pl.when(t < chunks)
         def _():
-            send_own(k + 2)
+            y_copy(0, left, t, y).wait_recv()
+            y_copy(2, left, t, right).start()
+            y_copy(1, right, t, y).wait_recv()
+            y_copy(3, right, t, left).start()
+
+        @pl.when(t + 2 < chunks)
+        def _():
+            send_own(t + 2)
 
         for number in range(1, N_EVENTS):
 
-            @pl.when(k == number)
+            @pl.when(t == number)
             def _(number=number):
                 for table in tables:
                     table.event(number)
 
-        lax.fori_loop(4, jnp.where(k == last, last - 1, 4), after_adapters, 0)
-        y_copy(2, across, k, y).wait_recv()
-        y_copy(3, across, k, y).wait_recv()
-        before_adapters(k)
-
-        @pl.when(k == TABLES_AT)
+        @pl.when(t > 0)
+        def _():
+            k = t - 1
+            y_copy(2, across, k, y).wait_recv()
+            y_copy(3, across, k, y).wait_recv()
+            before_adapters(k)
+
+        @pl.when(t == TABLES_AT)
         def _():
             for table in tables:
                 table.got_twins()
 
         lax.fori_loop(
-            jnp.where(k == TABLES_AT, 0, k), jnp.where(k >= TABLES_AT, k + 1, k), reduce_chunk, 0
+            jnp.where(t == TABLES_AT, 0, t - 1), jnp.where(t >= TABLES_AT, t, t - 1), reduce_chunk, 0
         )
         lax.fori_loop(
-            jnp.where(k == last, last - 1, 0),
-            jnp.where(k == last, chunks, jnp.where(k == last - 1, 4, 0)),
+            jnp.where(t == chunks, 4, 0),
+            jnp.where(t == chunks, chunks, jnp.where(t == last, 4, 0)),
             after_adapters,
             0,
         )
         return carry
 
-    lax.fori_loop(0, chunks, step, 0)
+    lax.fori_loop(0, chunks + 1, step, 0)
 
     for i in range(calls // CAP, sources):
         send_slots(i)
@@ -553,9 +562,10 @@
     call = jnp.arange(calls, dtype=jnp.int32)
     same = group[:, None] == group[None, :]
     rank = jnp.sum(jnp.where(same & (call[None, :] < call[:, None]), 1, 0), axis=1)
+    side = 1 - 2 * (me % 2)
     way = (
-        lax.rem(group // (2 * RING) - me // (2 * RING) + RING, RING) * (2 * RING)
-        + lax.rem((group // 2) % RING - (me // 2) % RING + RING, RING) * 2
+        lax.rem(side * (group // (2 * RING) - me // (2 * RING)) + RING, RING) * (2 * RING)
+        + lax.rem(side * ((group // 2) % RING - (me // 2) % RING) + RING, RING) * 2
         + lax.rem(group % 2 + me % 2, 2)
     )
     step_ways = jnp.array([dx * 2 * RING + dz * 2 + dc for dx, dz, dc in STEPS], jnp.int32)

time: 163 us -> 152 us (0.933)
  Pallas kernels: 146 us -> 137 us
    pallas_call x1, Pallas kernels: 146 us -> 137 us  [on_device(): pl.pallas_call(mixer_kernel, out_shape=jax.ShapeDtypeStruct((sources * CA...]
where the time goes in v3:
time: 152 us
  Pallas kernels  137 us (90%)
  local copies, waits for them, and re-layouts  8.71 us (6%)
  other arithmetic  6.05 us (4%)
    pallas_call x1, Pallas kernels, on_device(): pl.pallas_call(mixer_kernel, out_shape=jax.ShapeDtypeStruct((sources * CA...  137 us
    unnamed x4, local copies, waits for them, and re-layouts  7.23 us

profile of v3, /device:TPU:1, one launch (start us, length us, event | category | flops | bytes accessed | tf_op | source)
XLA Modules:
  0.0 151.6 jit_solution(193202770787121325)
XLA Ops:
  0.0 0.0 copy-start
  0.0 0.8 fusion.8
  0.8 0.0 copy-done
  0.8 0.1 dynamic-slice_bitcast_fusion
  0.9 0.8 select_reduce_fusion.3
  1.7 0.8 select_reduce_fusion.6
  2.6 0.2 select_reduce_fusion.5
  2.8 0.1 select_reduce_fusion.4
  2.9 0.1 select_reduce_fusion.1
  3.0 0.6 pad_add_fusion.meta
  3.6 1.3 select_maximum_fusion.params
  4.8 0.7 broadcast_in_dim.96
  5.6 0.7 reshape.34.skip
  6.2 1.3 maximum_convert_fusion.taps
  7.6 2.2 %copy.19.wdt_in = bf16[4096,16]{1,0:T(8,128)(2,1)} copy(bf16[4096,16]{0,1:T(8,128)(2,1)} %param.24) | data formatting | bytes 262144 | tf_op args[7]
  9.8 136.8 %shard_map.163 = bf16[64,32,1024]{2,1,0:T(8,128)(2,1)} custom-call(s32[4,64]{1,0:T(4,128)} %pad_add_fusion.meta, f32[8,128]{1,0:T(8,128)} %select_maximum_fusion.params, f32[4,1280]{1,0:T(4,128)} %maximum_convert_fusion.taps, f32[1,1024]{1,0:T(1,128)} %reshape.34.skip, bf16[4096,16]{1,0:T(8,128)(2,1)} %copy.19.wdt_in, bf16[32,32,1024]{2,1,0:T(8,128)(2,1)} %x_hbm.1, ...), custom_call_target="tpu_custom_call" | custom-call | flops 11811160064 | bytes 31457280 | tf_op jit(solution)/shard_map/pallas_call | solution.py:638
  146.6 5.0 %copy.21 = bf16[64,32,1024]{2,1,0:T(8,128)(2,1)} copy(bf16[64,32,1024]{2,1,0:T(8,128)(2,1)} %shard_map.163) | data formatting | bytes 8388608
  (2 shorter events, 0.0 us)
Async XLA Ops:
  0.0 0.8 copy-start

commit v4 on v3

--- a/solution.py
+++ b/solution.py
@@ -29,7 +29,8 @@
     ((0, 0),),
 )
 STEPS = tuple((dx, dz, dc) for group in CHIP_STEPS for dc in (1, 0) for dx, dz in group)
-TABLES_AT = 6
+TABLES_AT = 5
+FINISH = ((5, 0, 2), (6, 2, 5), (7, 5, 6), (8, 6, 8))
 
 
 def nt_dot(a, b):
@@ -171,9 +172,12 @@
 
 def mixer_kernel(
     meta,
-    params,
-    taps,
     skip,
+    decay_in,
+    bias_in,
+    x_taps,
+    b_taps,
+    c_taps,
     wdt_in,
     x_hbm,
     wx_hbm,
@@ -194,6 +198,8 @@
     low,
     gathered,
     slots,
+    params,
+    taps,
     load_sem,
     y_send,
     y_recv,
@@ -250,28 +256,14 @@
             device_id={"head": lax.rem(y + d, RING)},
             device_id_type=MESH,
         )
-    pl.semaphore_wait(barrier, sources - 1 + RING - 1)
-
-    table_down = Table(
-        down, table_send.at[0], table_recv.at[0], pos_x, pos_z, core, (2 * RING, 2), None
-    )
-    table_up = Table(
-        up, table_send.at[1], table_recv.at[1], pos_z, pos_x, core, (2, 2 * RING), None
-    )
-    tables = (table_down, table_up)
-
-    loads[1].wait()
-    loads[2].wait()
-    for table in tables:
-        table.event(0)
-
-    loads[0].wait()
 
     def arrange(j, carry):
         x_all[y, j] = x_in[meta[0, j]]
         return carry
 
-    lax.fori_loop(0, calls, arrange, 0)
+    loads[0].wait()
+    lax.fori_loop(0, 2 * CHUNK, arrange, 0)
+    pl.semaphore_wait(barrier, sources - 1 + RING - 1)
 
     def y_copy(kind, owner, k, target):
         if kind < 2:
@@ -294,12 +286,33 @@
     send_own(0)
     send_own(1)
 
+    table_down = Table(
+        down, table_send.at[0], table_recv.at[0], pos_x, pos_z, core, (2 * RING, 2), None
+    )
+    table_up = Table(
+        up, table_send.at[1], table_recv.at[1], pos_z, pos_x, core, (2, 2 * RING), None
+    )
+    tables = (table_down, table_up)
+    loads[1].wait()
+    loads[2].wait()
+    for table in tables:
+        table.event(0)
+    lax.fori_loop(2 * CHUNK, calls, arrange, 0)
+
+
     for c in range(CHUNK):
         between[c, pl.ds(0, PAD), :] = jnp.zeros((PAD, 2 * NSTATE), F32)
         for k in range(chunks):
             proj[k, c, pl.ds(0, PAD), :] = jnp.zeros((PAD, cols), F32)
     wdt[...] = jnp.zeros(wdt.shape, BF16)
-    wdt[:, pl.ds(0, wdt_in.shape[1])] = wdt_in[...]
+    heads = wdt_in.shape[0]
+    wdt[pl.ds(0, heads), :] = wdt_in[...]
+    params[...] = jnp.zeros(params.shape, F32)
+    params[0:1, pl.ds(0, heads)] = decay_in[...]
+    params[1:2, pl.ds(0, heads)] = bias_in[...]
+    taps[:, pl.ds(0, cols)] = x_taps[...].astype(F32)
+    taps[:, pl.ds(cols, NSTATE)] = b_taps[...].astype(F32)
+    taps[:, pl.ds(cols + NSTATE, NSTATE)] = c_taps[...].astype(F32)
     loads[3].wait()
     loads[4].wait()
     loads[5].wait()
@@ -346,7 +359,9 @@
         between[:, pl.ds(PAD, length), :] = project(
             k, w_all, pl.ds(cols, 2 * NSTATE)
         ).reshape(CHUNK, length, 2 * NSTATE)
-        raw = project(k, wdt, slice(None)) + bias
+        raw = bias
+        for owner in range(RING):
+            raw = raw + nt_dot(chunk_tokens(owner, k), wdt[:, pl.ds(owner * width, width)])
         t_iota = lax.broadcasted_iota(jnp.int32, (rows, rows), 0)
         j_iota = lax.broadcasted_iota(jnp.int32, (rows, rows), 1)
         causal = (t_iota // length == j_iota // length) & (j_iota <= t_iota)
@@ -468,7 +483,7 @@
             at = pl.ds(pair * 128, 128)
             x_conv = conv(proj.at[k], at, at)
             x_high = x_conv.astype(BF16)
-            mixed = skip[0:1, at] * x_conv
+            mixed = jnp.where(lane < HEAD_DIM, skip[2 * pair], skip[2 * pair + 1]) * x_conv
             for part in (x_high.astype(F32), x_conv - x_high.astype(F32)):
                 first = jnp.where(lane < HEAD_DIM, part, 0.0).astype(BF16)
                 second = jnp.where(lane < HEAD_DIM, 0.0, part).astype(BF16)
@@ -525,12 +540,11 @@
         lax.fori_loop(
             jnp.where(t == TABLES_AT, 0, t - 1), jnp.where(t >= TABLES_AT, t, t - 1), reduce_chunk, 0
         )
-        lax.fori_loop(
-            jnp.where(t == chunks, 4, 0),
-            jnp.where(t == chunks, chunks, jnp.where(t == last, 4, 0)),
-            after_adapters,
-            0,
-        )
+        first, end = 0, 0
+        for at, begin, until in FINISH:
+            first = jnp.where(t == at, begin, first)
+            end = jnp.where(t == at, until, end)
+        lax.fori_loop(first, end, after_adapters, 0)
         return carry
 
     lax.fori_loop(0, chunks + 1, step, 0)
@@ -623,12 +637,6 @@
     meta = routing(
         routed_group_index, call_adapter_index, holder_table_row, me, sources, calls
     )
-    params = jnp.stack([decay_logarithm, step_size_bias])
-    params = jnp.pad(params, ((0, 6), (0, 128 - heads)))
-    taps = jnp.concatenate(
-        [channel_input_taps, input_state_taps, output_state_taps], axis=1
-    ).astype(F32)
-    skip = jnp.broadcast_to(head_skip_factor[:, None], (heads, HEAD_DIM)).reshape(1, cols)
     down = jnp.swapaxes(adapter_down_weight, 1, 2)
     per_owner, rank, depth = down.shape
     rank_all = adapter_up_weight.shape[1]
@@ -638,13 +646,13 @@
     return pl.pallas_call(
         mixer_kernel,
         out_shape=jax.ShapeDtypeStruct((sources * CAP, length, cols), BF16),
-        in_specs=[pl.BlockSpec(memory_space=pltpu.SMEM)] + [vmem] * 4 + [anywhere] * 6,
+        in_specs=[pl.BlockSpec(memory_space=pltpu.SMEM)] * 2 + [vmem] * 6 + [anywhere] * 6,
         out_specs=anywhere,
         scratch_shapes=[
             pltpu.VMEM((calls, length, width), BF16),
             pltpu.VMEM((RING, calls, length, width), BF16),
             pltpu.VMEM((depth, total_cols), BF16),
-            pltpu.VMEM((depth, 128), BF16),
+            pltpu.VMEM((128, depth), BF16),
             pltpu.VMEM((sources, per_owner, rank, depth), BF16),
             pltpu.VMEM((sources, per_owner, rank_all, cols), BF16),
             pltpu.VMEM((chunks, CHUNK, PAD + length, cols), F32),
@@ -653,6 +661,8 @@
             pltpu.VMEM((RING, chunks, rows, 128), BF16),
             pltpu.VMEM((CHUNK * rank, depth), BF16),
             pltpu.VMEM((sources * CAP, length, cols), BF16),
+            pltpu.VMEM((8, 128), F32),
+            pltpu.VMEM((4, total_cols), F32),
             dma((7,)),
             dma((4, chunks)),
             dma((4, chunks)),
@@ -673,10 +683,13 @@
         ),
     )(
         meta,
-        params,
-        taps,
-        skip,
-        step_size_weight,
+        head_skip_factor,
+        decay_logarithm[None, :],
+        step_size_bias[None, :],
+        channel_input_taps,
+        input_state_taps,
+        output_state_taps,
+        step_size_weight.T,
         call_token_inputs,
         channel_input_weight,
         input_state_weight,

time: 152 us -> 139 us (0.914)
  Pallas kernels: 137 us -> 130 us
  local copies, waits for them, and re-layouts: 8.71 us -> 5.09 us
  other arithmetic: 6.05 us -> 3.45 us
    pallas_call x1, Pallas kernels: 137 us -> 130 us  [on_device(): pl.pallas_call(mixer_kernel, out_shape=jax.ShapeDtypeStruct((sources * CA...]
    unnamed x4 -> x3, local copies, waits for them, and re-layouts: 7.23 us -> 5.01 us
where the time goes in v4:
time: 139 us; the launch traced here: 138 us
  Pallas kernels  130 us (94%)
  local copies, waits for them, and re-layouts  5.09 us (4%)
  other arithmetic  3.45 us (2%)
    pallas_call x1, Pallas kernels, on_device(): pl.pallas_call(mixer_kernel, out_shape=jax.ShapeDtypeStruct((sources * CA...  130 us
    unnamed x3, local copies, waits for them, and re-layouts  5.01 us

profile of v4, /device:TPU:1, one launch (start us, length us, event | category | flops | bytes accessed | tf_op | source)
XLA Modules:
  0.0 138.4 jit_solution(18394453157512503730)
XLA Ops:
  0.0 0.0 copy-start
  0.0 0.8 fusion.8
  0.8 0.0 copy-done
  0.8 0.1 dynamic-slice_bitcast_fusion
  0.9 0.8 select_reduce_fusion.3
  1.7 0.8 select_reduce_fusion.6
  2.6 0.2 select_reduce_fusion.5
  2.8 0.1 select_reduce_fusion.4
  2.9 0.1 select_reduce_fusion.1
  3.0 0.6 pad_add_fusion.meta
  3.6 129.8 %shard_map.163 = bf16[64,32,1024]{2,1,0:T(8,128)(2,1)} custom-call(s32[4,64]{1,0:T(4,128)} %pad_add_fusion.meta, f32[16]{0:T(128)} %skip.1, f32[1,16]{1,0:T(1,128)} %bitcast.16, f32[1,16]{1,0:T(1,128)} %bitcast.17, bf16[4,1024]{1,0:T(4,128)(2,1)} %x_taps.1, bf16[4,128]{1,0:T(4,128)(2,1)} %b_taps.1, bf16[4,128]{1,0:T(4,128)(2,1)} %c_taps.1, ...), custom_call_target="tpu_custom_call" | custom-call | flops 11811160064 | bytes 31457280 | tf_op jit(solution)/shard_map/pallas_call | solution.py:646
  133.3 5.0 %copy.19 = bf16[64,32,1024]{2,1,0:T(8,128)(2,1)} copy(bf16[64,32,1024]{2,1,0:T(8,128)(2,1)} %shard_map.163) | data formatting | bytes 8388608
  (2 shorter events, 0.0 us)
Async XLA Ops:
  0.0 0.8 copy-start

commit v5 on v4

--- a/solution.py
+++ b/solution.py
@@ -29,8 +29,8 @@
     ((0, 0),),
 )
 STEPS = tuple((dx, dz, dc) for group in CHIP_STEPS for dc in (1, 0) for dx, dz in group)
-TABLES_AT = 5
-FINISH = ((5, 0, 2), (6, 2, 5), (7, 5, 6), (8, 6, 8))
+TABLES_AT = 4
+FINISH = ((4, 0, 2), (5, 2, 4), (6, 4, 5), (7, 5, 6), (8, 6, 8))
 
 
 def nt_dot(a, b):
@@ -518,7 +518,7 @@
         def _():
             send_own(t + 2)
 
-        for number in range(1, N_EVENTS):
+        for number in range(1, TABLES_AT + 1):
 
             @pl.when(t == number)
             def _(number=number):
@@ -534,6 +534,9 @@
 
         @pl.when(t == TABLES_AT)
         def _():
+            for number in range(TABLES_AT + 1, N_EVENTS):
+                for table in tables:
+                    table.event(number)
             for table in tables:
                 table.got_twins()
 

time: 139 us -> 131 us (0.942)
  Pallas kernels: 130 us -> 121 us
    pallas_call x1, Pallas kernels: 130 us -> 121 us  [on_device(): pl.pallas_call(mixer_kernel, out_shape=jax.ShapeDtypeStruct((sources * CA...]
where the time goes in v5:
time: 131 us; the launch traced here: 130 us
  Pallas kernels  121 us (92%)
  local copies, waits for them, and re-layouts  5.09 us (4%)
  other arithmetic  3.45 us (3%)
    pallas_call x1, Pallas kernels, on_device(): pl.pallas_call(mixer_kernel, out_shape=jax.ShapeDtypeStruct((sources * CA...  121 us
    unnamed x3, local copies, waits for them, and re-layouts  5.01 us

profile of v5, /device:TPU:1, one launch (start us, length us, event | category | flops | bytes accessed | tf_op | source)
XLA Modules:
  0.0 129.8 jit_solution(14242340650407783907)
XLA Ops:
  0.0 0.0 copy-start
  0.0 0.8 fusion.8
  0.8 0.0 copy-done
  0.8 0.1 dynamic-slice_bitcast_fusion
  0.9 0.8 select_reduce_fusion.3
  1.7 0.8 select_reduce_fusion.6
  2.6 0.2 select_reduce_fusion.5
  2.8 0.1 select_reduce_fusion.4
  2.9 0.1 select_reduce_fusion.1
  3.0 0.6 pad_add_fusion.meta
  3.6 121.2 %shard_map.163 = bf16[64,32,1024]{2,1,0:T(8,128)(2,1)} custom-call(s32[4,64]{1,0:T(4,128)} %pad_add_fusion.meta, f32[16]{0:T(128)} %skip.1, f32[1,16]{1,0:T(1,128)} %bitcast.16, f32[1,16]{1,0:T(1,128)} %bitcast.17, bf16[4,1024]{1,0:T(4,128)(2,1)} %x_taps.1, bf16[4,128]{1,0:T(4,128)(2,1)} %b_taps.1, bf16[4,128]{1,0:T(4,128)(2,1)} %c_taps.1, ...), custom_call_target="tpu_custom_call" | custom-call | flops 11811160064 | bytes 31457280 | tf_op jit(solution)/shard_map/pallas_call | solution.py:649
  124.7 5.0 %copy.19 = bf16[64,32,1024]{2,1,0:T(8,128)(2,1)} copy(bf16[64,32,1024]{2,1,0:T(8,128)(2,1)} %shard_map.163) | data formatting | bytes 8388608
  (2 shorter events, 0.0 us)
Async XLA Ops:
  0.0 0.8 copy-start

commit v6 on v5

--- a/solution.py
+++ b/solution.py
@@ -326,12 +326,12 @@
     def chunk_tokens(owner, k):
         return x_all[owner, pl.ds(k * CHUNK, CHUNK)].reshape(rows, width)
 
-    def project(k, weight, at):
+    def project(k, weight, at, owners=(0, 1, 2, 3)):
         total = None
-        for owner in range(RING):
+        for owner in owners:
             term = jnp.dot(
                 chunk_tokens(owner, k),
-                weight[pl.ds(owner * width, width), at],
+                weight[pl.ds(pl.multiple_of(owner * width, width), width), at],
                 preferred_element_type=F32,
             )
             total = term if total is None else total + term
@@ -346,15 +346,23 @@
         total = total.reshape(rows, 128)
         return total / (1.0 + jnp.exp(-total))
 
-    def before_adapters(k):
-        tile = 256 if cols % 256 == 0 else 128
-
+    tile = 256 if cols % 256 == 0 else 128
+
+    def project_near(k):
         @pl.loop(0, cols // tile)
         def _(n):
             at = pl.ds(pl.multiple_of(n * tile, tile), tile)
-            proj[k, :, pl.ds(PAD, length), at] = project(k, w_all, at).reshape(
-                CHUNK, length, tile
-            )
+            proj[k, :, pl.ds(PAD, length), at] = project(
+                k, w_all, at, (y, left, right)
+            ).reshape(CHUNK, length, tile)
+
+    def before_adapters(k):
+        @pl.loop(0, cols // tile)
+        def _(n):
+            at = pl.ds(pl.multiple_of(n * tile, tile), tile)
+            proj[k, :, pl.ds(PAD, length), at] = proj[
+                k, :, pl.ds(PAD, length), at
+            ] + project(k, w_all, at, (across,)).reshape(CHUNK, length, tile)
 
         between[:, pl.ds(PAD, length), :] = project(
             k, w_all, pl.ds(cols, 2 * NSTATE)
@@ -514,10 +522,6 @@
             y_copy(1, right, t, y).wait_recv()
             y_copy(3, right, t, left).start()
 
-        @pl.when(t + 2 < chunks)
-        def _():
-            send_own(t + 2)
-
         for number in range(1, TABLES_AT + 1):
 
             @pl.when(t == number)
@@ -527,10 +531,18 @@
 
         @pl.when(t > 0)
         def _():
-            k = t - 1
-            y_copy(2, across, k, y).wait_recv()
-            y_copy(3, across, k, y).wait_recv()
-            before_adapters(k)
+            y_copy(2, across, t - 1, y).wait_recv()
+            y_copy(3, across, t - 1, y).wait_recv()
+
+        lax.fori_loop(jnp.where(t > TABLES_AT, t - 1, t), t, reduce_chunk, 0)
+
+        @pl.when(t + 2 < chunks)
+        def _():
+            send_own(t + 2)
+
+        @pl.when(t > 0)
+        def _():
+            before_adapters(t - 1)
 
         @pl.when(t == TABLES_AT)
         def _():
@@ -540,14 +552,17 @@
             for table in tables:
                 table.got_twins()
 
-        lax.fori_loop(
-            jnp.where(t == TABLES_AT, 0, t - 1), jnp.where(t >= TABLES_AT, t, t - 1), reduce_chunk, 0
-        )
+        lax.fori_loop(0, jnp.where(t == TABLES_AT, t, 0), reduce_chunk, 0)
         first, end = 0, 0
         for at, begin, until in FINISH:
             first = jnp.where(t == at, begin, first)
             end = jnp.where(t == at, until, end)
         lax.fori_loop(first, end, after_adapters, 0)
+
+        @pl.when(t < chunks)
+        def _():
+            project_near(t)
+
         return carry
 
     lax.fori_loop(0, chunks + 1, step, 0)
@@ -648,9 +663,9 @@
     dma = pltpu.SemaphoreType.DMA
     return pl.pallas_call(
         mixer_kernel,
-        out_shape=jax.ShapeDtypeStruct((sources * CAP, length, cols), BF16),
+        out_shape=pltpu.VMEM((sources * CAP, length, cols), BF16),
         in_specs=[pl.BlockSpec(memory_space=pltpu.SMEM)] * 2 + [vmem] * 6 + [anywhere] * 6,
-        out_specs=anywhere,
+        out_specs=pl.BlockSpec(memory_space=pl.ANY),
         scratch_shapes=[
             pltpu.VMEM((calls, length, width), BF16),
             pltpu.VMEM((RING, calls, length, width), BF16),
@@ -677,7 +692,7 @@
             dma((sources,)),
         ],
         compiler_params=pltpu.CompilerParams(
-            collective_id=0, has_side_effects=True, vmem_limit_bytes=60 * 2**20
+            collective_id=0, has_side_effects=True, vmem_limit_bytes=56 * 2**20
         ),
         cost_estimate=pl.CostEstimate(
             flops=2 * calls * length * depth * (total_cols + 128),

time: 131 us -> 126 us (0.962); the launches traced: 130 us -> 126 us
  local copies, waits for them, and re-layouts: 5.09 us -> 2.1 us
    unnamed x3, local copies, waits for them, and re-layouts: 5.01 us -> 2.02 us
where the time goes in v6:
time: 126 us
  Pallas kernels  121 us (96%)
  other arithmetic  3.45 us (3%)
  local copies, waits for them, and re-layouts  2.1 us (2%)
    pallas_call x1, Pallas kernels, on_device(): pl.pallas_call(mixer_kernel, out_shape=pltpu.VMEM((sources * CAP, length,...  121 us

profile of v6, /device:TPU:1, one launch (start us, length us, event | category | flops | bytes accessed | tf_op | source)
XLA Modules:
  0.0 126.2 jit_solution(10252423215416985405)
XLA Ops:
  0.0 0.0 copy-start
  0.0 0.8 fusion.8
  0.8 0.0 copy-done
  0.8 0.1 dynamic-slice_bitcast_fusion
  0.9 0.8 select_reduce_fusion.3
  1.7 0.8 select_reduce_fusion.6
  2.6 0.2 select_reduce_fusion.5
  2.8 0.1 select_reduce_fusion.4
  2.9 0.1 select_reduce_fusion.1
  3.0 0.6 pad_add_fusion.meta
  3.6 120.6 %shard_map.163 = bf16[64,32,1024]{2,1,0:T(8,128)(2,1)S(1)} custom-call(s32[4,64]{1,0:T(4,128)} %pad_add_fusion.meta, f32[16]{0:T(128)} %skip.1, f32[1,16]{1,0:T(1,128)} %bitcast.16, f32[1,16]{1,0:T(1,128)} %bitcast.17, bf16[4,1024]{1,0:T(4,128)(2,1)} %x_taps.1, bf16[4,128]{1,0:T(4,128)(2,1)} %b_taps.1, bf16[4,128]{1,0:T(4,128)(2,1)} %c_taps.1, ...), custom_call_target="tpu_custom_call" | custom-call | flops 11811160064 | bytes 31457280 | tf_op jit(solution)/shard_map/pallas_call | solution.py:664
  124.1 2.0 %copy.19 = bf16[64,32,1024]{2,1,0:T(8,128)(2,1)} copy(bf16[64,32,1024]{2,1,0:T(8,128)(2,1)S(1)} %shard_map.163) | data formatting | bytes 8388608
  (2 shorter events, 0.0 us)
Async XLA Ops:
  0.0 0.8 copy-start

commit v7 on v6

--- a/solution.py
+++ b/solution.py
@@ -28,7 +28,40 @@
     ((1, 0), (3, 0), (0, 1), (0, 3)),
     ((0, 0),),
 )
-STEPS = tuple((dx, dz, dc) for group in CHIP_STEPS for dc in (1, 0) for dx, dz in group)
+STEPS = (
+    (2, 1, 1),
+    (2, 3, 1),
+    (1, 2, 1),
+    (3, 2, 1),
+    (2, 1, 0),
+    (2, 3, 0),
+    (1, 2, 0),
+    (3, 2, 0),
+    (2, 2, 1),
+    (2, 0, 1),
+    (0, 2, 1),
+    (2, 2, 0),
+    (2, 0, 0),
+    (0, 2, 0),
+    (1, 1, 1),
+    (3, 3, 1),
+    (0, 0, 1),
+    (0, 0, 0),
+    (1, 0, 1),
+    (3, 0, 1),
+    (0, 1, 1),
+    (0, 3, 1),
+    (1, 3, 1),
+    (3, 1, 1),
+    (1, 1, 0),
+    (3, 3, 0),
+    (1, 3, 0),
+    (3, 1, 0),
+    (1, 0, 0),
+    (3, 0, 0),
+    (0, 1, 0),
+    (0, 3, 0),
+)
 TABLES_AT = 4
 FINISH = ((4, 0, 2), (5, 2, 4), (6, 4, 5), (7, 5, 6), (8, 6, 8))
 
@@ -234,7 +267,7 @@
             wc_hbm, w_all.at[:, pl.ds(cols + NSTATE, NSTATE)], load_sem.at[5]
         ),
     ]
-    for load in loads:
+    for load in loads[:3]:
         load.start()
 
     barrier = pltpu.get_barrier_semaphore()
@@ -297,6 +330,8 @@
     loads[2].wait()
     for table in tables:
         table.event(0)
+    for load in loads[3:]:
+        load.start()
     lax.fori_loop(2 * CHUNK, calls, arrange, 0)
 
 
@@ -592,22 +627,18 @@
     group = lax.dynamic_slice(routed_group_index, (me * calls,), (calls,))
     named = lax.dynamic_slice(call_adapter_index[:, 0], (me * calls,), (calls,))
     call = jnp.arange(calls, dtype=jnp.int32)
-    same = group[:, None] == group[None, :]
-    rank = jnp.sum(jnp.where(same & (call[None, :] < call[:, None]), 1, 0), axis=1)
     side = 1 - 2 * (me % 2)
     way = (
-        lax.rem(side * (group // (2 * RING) - me // (2 * RING)) + RING, RING) * (2 * RING)
-        + lax.rem(side * ((group // 2) % RING - (me // 2) % RING) + RING, RING) * 2
-        + lax.rem(group % 2 + me % 2, 2)
-    )
-    step_ways = jnp.array([dx * 2 * RING + dz * 2 + dc for dx, dz, dc in STEPS], jnp.int32)
-    step = jnp.sum(
-        jnp.where(
-            way[:, None] == step_ways[None, :], jnp.arange(sources, dtype=jnp.int32)[None, :], 0
-        ),
-        axis=1,
-    )
-    key = step * CAP + rank
+        lax.rem(side * (lax.shift_right_logical(group, 3) - me // (2 * RING)) + RING, RING)
+        * (2 * RING)
+        + lax.rem(side * ((lax.shift_right_logical(group, 1) & 3) - (me // 2) % RING) + RING, RING)
+        * 2
+        + ((group + me) & 1)
+    )
+    step = jnp.zeros((calls,), jnp.int32)
+    for i, (dx, dz, dc) in enumerate(STEPS):
+        step = jnp.where(way == dx * 2 * RING + dz * 2 + dc, i, step)
+    key = step * calls + call
     place = jnp.sum(jnp.where(key[None, :] < key[:, None], 1, 0), axis=1)
     row = jnp.sum(
         jnp.where(
@@ -621,8 +652,11 @@
     here = place[None, :] == slot[:, None]
     order = jnp.sum(jnp.where(here, call[None, :], 0), axis=1)
     rows = jnp.sum(jnp.where(here, row[None, :], 0), axis=1)
-    taken = jnp.sum(jnp.where(key[None, :] < slot[:, None], 1, 0), axis=1)
-    live = jnp.sum(jnp.where(key[None, :] == slot[:, None], 1, 0), axis=1)
+    slot_step, slot_rank = slot // CAP, slot % CAP
+    ahead = jnp.sum(jnp.where(step[None, :] < slot_step[:, None], 1, 0), axis=1)
+    count = jnp.sum(jnp.where(step[None, :] == slot_step[:, None], 1, 0), axis=1)
+    taken = ahead + jnp.minimum(slot_rank, count)
+    live = jnp.where(count > slot_rank, 1, 0)
     return jnp.stack([order, rows, jnp.minimum(taken, calls - 1), live]).astype(jnp.int32)
 
 

time: 126 us -> 125 us (level)
  no operation moved by 1% of the time
where the time goes in v7:
time: 125 us
  Pallas kernels  120 us (96%)
  other arithmetic  2.61 us (2%)
  local copies, waits for them, and re-layouts  2.1 us (2%)
    pallas_call x1, Pallas kernels, on_device(): pl.pallas_call(mixer_kernel, out_shape=pltpu.VMEM((sources * CAP, length,...  120 us

profile of v7, /device:TPU:1, one launch (start us, length us, event | category | flops | bytes accessed | tf_op | source)
XLA Modules:
  0.0 125.2 jit_solution(9833478157777305269)
XLA Ops:
  0.0 0.0 copy-start
  0.0 0.8 iota_add_fusion
  0.8 0.0 copy-done
  0.8 0.1 dynamic-slice_bitcast_fusion
  0.9 0.8 select_reduce_fusion.3
  1.7 0.2 select_reduce_fusion.5
  1.9 0.1 select_reduce_fusion.4
  2.0 0.1 select_reduce_fusion.1
  2.1 0.6 pad_add_fusion.meta
  2.7 120.4 %shard_map.154 = bf16[64,32,1024]{2,1,0:T(8,128)(2,1)S(1)} custom-call(s32[4,64]{1,0:T(4,128)} %pad_add_fusion.meta, f32[16]{0:T(128)} %skip.1, f32[1,16]{1,0:T(1,128)} %bitcast.21, f32[1,16]{1,0:T(1,128)} %bitcast.22, bf16[4,1024]{1,0:T(4,128)(2,1)} %x_taps.1, bf16[4,128]{1,0:T(4,128)(2,1)} %b_taps.1, bf16[4,128]{1,0:T(4,128)(2,1)} %c_taps.1, ...), custom_call_target="tpu_custom_call" | custom-call | flops 11811160064 | bytes 31457280 | tf_op jit(solution)/shard_map/pallas_call | solution.py:698
  123.2 2.0 %copy.18 = bf16[64,32,1024]{2,1,0:T(8,128)(2,1)} copy(bf16[64,32,1024]{2,1,0:T(8,128)(2,1)S(1)} %shard_map.154) | data formatting | bytes 8388608
  (2 shorter events, 0.0 us)
Async XLA Ops:
  0.0 0.8 copy-start

commit v8 on v7

--- a/solution.py
+++ b/solution.py
@@ -333,6 +333,7 @@
     for load in loads[3:]:
         load.start()
     lax.fori_loop(2 * CHUNK, calls, arrange, 0)
+    send_own(2)
 
 
     for c in range(CHUNK):
@@ -571,9 +572,9 @@
 
         lax.fori_loop(jnp.where(t > TABLES_AT, t - 1, t), t, reduce_chunk, 0)
 
-        @pl.when(t + 2 < chunks)
+        @pl.when(t + 3 < chunks)
         def _():
-            send_own(t + 2)
+            send_own(t + 3)
 
         @pl.when(t > 0)
         def _():

time: 125 us -> 132 us (1.056)
  Pallas kernels: 120 us -> 127 us
    pallas_call x1, Pallas kernels: 120 us -> 127 us  [on_device(): pl.pallas_call(mixer_kernel, out_shape=pltpu.VMEM((sources * CAP, length,...]
where the time goes in v8:
time: 132 us; the launch traced here: 131 us
  Pallas kernels  127 us (96%)
  other arithmetic  2.61 us (2%)
  local copies, waits for them, and re-layouts  2.1 us (2%)
    pallas_call x1, Pallas kernels, on_device(): pl.pallas_call(mixer_kernel, out_shape=pltpu.VMEM((sources * CAP, length,...  127 us

profile of v8, /device:TPU:1, one launch (start us, length us, event | category | flops | bytes accessed | tf_op | source)
XLA Modules:
  0.0 131.5 jit_solution(12794735330069112775)
XLA Ops:
  0.0 0.0 copy-start
  0.0 0.8 iota_add_fusion
  0.8 0.0 copy-done
  0.8 0.1 dynamic-slice_bitcast_fusion
  0.9 0.8 select_reduce_fusion.3
  1.7 0.2 select_reduce_fusion.5
  1.9 0.1 select_reduce_fusion.4
  2.0 0.1 select_reduce_fusion.1
  2.1 0.6 pad_add_fusion.meta
  2.7 126.7 %shard_map.154 = bf16[64,32,1024]{2,1,0:T(8,128)(2,1)S(1)} custom-call(s32[4,64]{1,0:T(4,128)} %pad_add_fusion.meta, f32[16]{0:T(128)} %skip.1, f32[1,16]{1,0:T(1,128)} %bitcast.21, f32[1,16]{1,0:T(1,128)} %bitcast.22, bf16[4,1024]{1,0:T(4,128)(2,1)} %x_taps.1, bf16[4,128]{1,0:T(4,128)(2,1)} %b_taps.1, bf16[4,128]{1,0:T(4,128)(2,1)} %c_taps.1, ...), custom_call_target="tpu_custom_call" | custom-call | flops 11811160064 | bytes 31457280 | tf_op jit(solution)/shard_map/pallas_call | solution.py:699
  129.4 2.0 %copy.18 = bf16[64,32,1024]{2,1,0:T(8,128)(2,1)} copy(bf16[64,32,1024]{2,1,0:T(8,128)(2,1)S(1)} %shard_map.154) | data formatting | bytes 8388608
  (2 shorter events, 0.0 us)
Async XLA Ops:
  0.0 0.8 copy-start
